TPU v7x, 512 devices: a whole 4x8x8 slice. The times are simulated.
512 devices in a mesh: ctx: 32 (over y, x), tp: 16 (over z, core).
Axes of the slice: x: 4, y: 8, z: 8, core: 2. Of those that a mesh axis runs over, the one named last changes fastest.
Arguments:
- hidden_states: bfloat16 [8192, 8192], P('ctx', 'tp'), may hold values from -6 to 6
- ssm_input: bfloat16 [8192, 16384], P('ctx', 'tp'), may hold values from -6 to 6
- step_size: float32 [256, 8192], P('tp', 'ctx'), may hold values from 0.25 to 73728
- decay_rate: float32 [256], P('tp'), may hold values from 6.1035156e-06 to 0.05
- proj_b: bfloat16 [16, 8192], P(None, 'ctx'), may hold values from -1.5 to 1.5
- proj_c: bfloat16 [16, 8192], P(None, 'ctx'), may hold values from -1.5 to 1.5
- skip_gain: float32 [256], P('tp'), may hold values from 0.5 to 2
- norm_gain: float32 [16384], P('tp'), may hold values from 0.5 to 1.5
- latent_from_ssm: bfloat16 [16384, 256], P('tp'), may hold values from -0.03125 to 0.03125
- latent_from_hidden: bfloat16 [8192, 256], P('tp'), may hold values from -0.046875 to 0.046875
- key_rebuild: bfloat16 [256, 1024], replicated, may hold values from -0.375 to 0.375
- value_rebuild: bfloat16 [256, 1024], replicated, may hold values from -0.375 to 0.375
- queries: bfloat16 [8192, 8192], P('ctx', 'tp'), may hold values from -720 to 720
Outputs:
- mamba_out: bfloat16 [8192, 16384], P('ctx', 'tp')
- attended: bfloat16 [8192, 8192], P('ctx', 'tp')
All inputs are finite; a program needn't handle non-finite values.
Results may differ from a plain program's by a relative error of at most 0.035.
Values may be sent and summed in bfloat16 or wider, within the bound.
No kernel may reach another device: no remote copies, remote signals or barrier semaphores. Data moves between devices by JAX's collectives and lax.ppermute only.
A program may use at most 64 MiB of HBM per device.

v0:
```python
import math

import jax
import jax.numpy as jnp
from jax import lax
from jax.sharding import PartitionSpec as P

STATE = 16
HEADDIM = 64
STRETCH = 256
HD = 128
GROUP = 8


NEG_BIG = -1e30
EPSILON = 1e-05
HIGHEST = lax.Precision.HIGHEST


def carried_in(value, axis, join, neutral):
    count, mine = (lax.axis_size(axis), lax.axis_index(axis))
    pieces = jax.tree.map(lambda part: lax.all_gather(part, axis), value)
    subtotal = jax.tree.map(
        lambda part, zero: jnp.full_like(part, 0) + jnp.asarray(zero, part.dtype), value, neutral
    )

    def lap(position, subtotal):
        longer = join(subtotal, jax.tree.map(lambda part: part[position], pieces))
        return jax.tree.map(lambda new, old: jnp.where(position < mine, new, old), longer, subtotal)

    return lax.fori_loop(0, count - 1, lap, subtotal)


def join_states(earlier, later):
    return (earlier[0] + later[0], jnp.exp(later[0])[:, None, None] * earlier[1] + later[1])


def body(
    hidden_states,
    ssm_input,
    step_size,
    decay_rate,
    proj_b,
    proj_c,
    skip_gain,
    norm_gain,
    latent_from_ssm,
    latent_from_hidden,
    key_rebuild,
    value_rebuild,
    queries,
):
    row_count = ssm_input.shape[0]
    inner_local = ssm_input.shape[1]
    head_count = inner_local // HEADDIM
    block_count = row_count // STRETCH
    log_step = -decay_rate[:, None] * step_size
    within = jnp.cumsum(log_step.reshape(head_count, block_count, STRETCH), axis=2)
    block_logs = within[:, :, -1]
    before = jnp.cumsum(block_logs, axis=1) - block_logs
    causal = jnp.arange(STRETCH)[:, None] >= jnp.arange(STRETCH)[None, :]
    x_blocks = ssm_input.reshape(block_count, STRETCH, head_count, HEADDIM)
    b_blocks = proj_b.reshape(STATE, block_count, STRETCH)
    c_blocks = proj_c.reshape(STATE, block_count, STRETCH)
    intersection = jnp.einsum(
        "nct,ncs->cts", c_blocks, b_blocks, preferred_element_type=jnp.float32
    )
    gaps = within[:, :, :, None] - within[:, :, None, :]
    decays = jnp.where(causal, jnp.exp(jnp.where(causal, gaps, 0.0)), 0.0)
    mixing = (intersection[None] * decays).astype(jnp.bfloat16)
    intra = jnp.einsum("hcts,cshp->cthp", mixing, x_blocks, preferred_element_type=jnp.float32)
    to_end = jnp.exp(block_logs[:, :, None] - within)
    weighted = x_blocks.astype(jnp.float32) * jnp.transpose(to_end, (1, 2, 0))[:, :, :, None]
    fresh_states = jnp.einsum(
        "cshp,ncs->chpn", weighted, b_blocks.astype(jnp.float32), precision=HIGHEST
    )

    def advance(carried, element):
        block_log, fresh_state = element
        return (jnp.exp(block_log)[:, None, None] * carried + fresh_state, carried)

    empty_state = jnp.zeros((head_count, HEADDIM, STATE), jnp.float32)
    local_end, entering = lax.scan(advance, empty_state, (block_logs.T, fresh_states))
    device_log = jnp.sum(block_logs, axis=1)
    identity = (jnp.zeros((head_count,), jnp.float32), empty_state)
    _, arriving = carried_in((device_log, local_end), "ctx", join_states, identity)
    full_entering = entering + jnp.exp(before.T)[:, :, None, None] * arriving[None]
    from_state = jnp.einsum(
        "nct,chpn->cthp", c_blocks.astype(jnp.float32), full_entering, precision=HIGHEST
    )
    growth = jnp.transpose(jnp.exp(within), (1, 2, 0))[:, :, :, None]
    ssm_out = (
        intra + from_state * growth + skip_gain[None, None, :, None] * x_blocks.astype(jnp.float32)
    )
    square_mean = jnp.mean(ssm_out * ssm_out, axis=-1, keepdims=True)
    normalized = ssm_out * lax.rsqrt(square_mean + EPSILON)
    mamba_out = (normalized.reshape(row_count, inner_local) * norm_gain[None, :]).astype(
        jnp.bfloat16
    )
    latent_terms = jnp.dot(mamba_out, latent_from_ssm, preferred_element_type=jnp.float32)
    latent_terms = latent_terms + jnp.dot(
        hidden_states, latent_from_hidden, preferred_element_type=jnp.float32
    )
    latents = lax.psum(latent_terms, "tp").astype(jnp.bfloat16)
    heads_query = queries.shape[1] // HD
    kv_local = max(1, heads_query // GROUP)
    per_kv = heads_query // kv_local
    kv_first = lax.axis_index("tp") * heads_query // GROUP
    key_columns = lax.dynamic_slice_in_dim(key_rebuild, kv_first * HD, kv_local * HD, 1)
    value_columns = lax.dynamic_slice_in_dim(value_rebuild, kv_first * HD, kv_local * HD, 1)
    query_first = lax.axis_index("ctx") * row_count
    scale = 1.0 / math.sqrt(HD)
    query_sets = [(queries, query_first + jnp.arange(row_count, dtype=jnp.int32))]
    groups = [
        (rows_set.reshape(rows_set.shape[0], kv_local, per_kv, HD), positions, positions[-1])
        for rows_set, positions in query_sets
    ]
    final_any = groups[0][2]

    def absorb(running, grouped, positions, key_blk, value_blk, first_key):
        best, norm_sum, accum = running
        width = key_blk.shape[0]
        scores = (
            jnp.einsum("tkgd,skd->kgts", grouped, key_blk, preferred_element_type=jnp.float32)
            * scale
        )
        allowed = (first_key + jnp.arange(width, dtype=jnp.int32))[None, :] <= positions[:, None]
        scores = jnp.where(allowed, scores, -jnp.inf)
        new_best = jnp.maximum(best, jnp.max(scores, axis=-1))
        factor = jnp.exp(best - new_best)
        weights = jnp.exp(scores - new_best[..., None])
        norm_sum = norm_sum * factor + jnp.sum(weights, axis=-1)
        accum = accum * factor[..., None] + jnp.einsum(
            "kgts,skd->kgtd",
            weights.astype(jnp.bfloat16),
            value_blk,
            preferred_element_type=jnp.float32,
        )
        return (new_best, norm_sum, accum)

    def from_latents(portion, begin, width):
        latent_blk = lax.dynamic_slice_in_dim(portion, begin, width, 0)
        key_blk = jnp.dot(latent_blk, key_columns, preferred_element_type=jnp.float32).astype(
            jnp.bfloat16
        )
        value_blk = jnp.dot(latent_blk, value_columns, preferred_element_type=jnp.float32).astype(
            jnp.bfloat16
        )
        return (key_blk.reshape(width, kv_local, HD), value_blk.reshape(width, kv_local, HD))

    starting = tuple(
        (
            (
                jnp.full((kv_local, per_kv, entry[0].shape[0]), NEG_BIG, jnp.float32),
                jnp.zeros((kv_local, per_kv, entry[0].shape[0]), jnp.float32),
                jnp.zeros((kv_local, per_kv, entry[0].shape[0], HD), jnp.float32),
            )
            for entry in groups
        )
    )
    portion = lax.all_gather(latents, "ctx", axis=0, tiled=True)
    length = portion.shape[0]
    key_block = math.gcd(length, 512)

    def visit(number, carried):
        first_key = number * key_block

        def work(current):
            key_blk, value_blk = from_latents(portion, number * key_block, key_block)
            updated = []
            for entry, state in zip(groups, current):

                def absorb_one(state_now, entry=entry):
                    return absorb(state_now, entry[0], entry[1], key_blk, value_blk, first_key)

                updated.append(
                    lax.cond(first_key <= entry[2], absorb_one, lambda unchanged: unchanged, state)
                )
            return tuple(updated)

        return lax.cond(first_key <= final_any, work, lambda unchanged: unchanged, carried)

    finished = lax.fori_loop(0, length // key_block, visit, starting)
    outputs = []
    for state in finished:
        result = state[2] / state[1][..., None]
        count_rows = result.shape[2]
        outputs.append(
            jnp.transpose(result, (2, 0, 1, 3))
            .reshape(count_rows, heads_query * HD)
            .astype(jnp.bfloat16)
        )
    attended = outputs[0]
    return (mamba_out, attended)


def solution(mesh):
    return jax.shard_map(
        body,
        mesh=mesh,
        in_specs=(
            P("ctx", "tp"),
            P("ctx", "tp"),
            P("tp", "ctx"),
            P("tp"),
            P(None, "ctx"),
            P(None, "ctx"),
            P("tp"),
            P("tp"),
            P("tp", None),
            P("tp", None),
            P(),
            P(),
            P("ctx", "tp"),
        ),
        out_specs=(P("ctx", "tp"), P("ctx", "tp")),
        check_vma=False,
    )
```

profile of v0, /device:TPU:60, one launch (start us, length us, event | category | flops | bytes accessed | tf_op | source)
XLA Modules:
  0.0 366.1 jit_solution(12062932581427749813)
XLA Ops:
  15.2 70.6 %all-reduce = f32[512]{0:T(512)S(1)} all-reduce(f32[512]{0:T(512)S(1)} %dynamic-update-slice), channel_id=2, replica_groups=mesh['ctx'=32,'tp'=16] {'ctx'}, use_global_device_ids=true, to_apply=%add | all-reduce | flops 512 | bytes 4096
  86.2 16.2 %all-gather.7.cloned.1.call-done = f32[512,64,16]{1,2,0:T(8,128)} async-done(((f32[16,64,16]{1,2,0:T(8,128)}), f32[512,64,16]{1,2,0:T(8,128)}) %all-gather.7.cloned.1.call-update) | async-done | bytes 2097168 | tf_op jit(solution)/shard_map/all_gather | solution.py:22
  102.3 32.3 %while.38 = (s32[]{:T(128)}, f32[16,64,16]{1,2,0:T(8,128)S(1)}, s32[]{:T(128)}, f32[32,16]{1,0:T(8,128)S(1)}, f32[32,16,64,16]{2,3,1,0:T(8,128)}, /*index=5*/s32[]{:T(128)}, s32[]{:T(128)}) while((s32[]{:T(128)}, f32[16,64,16]{1,2,0:T(8,128)S(1)}, s32[]{:T(128)}, f32[32,16]{1,0:T(8,128)S(1)}, f32[32,16,64,16]{2,3,1,0:T(8,128)}, ...), condition=%wide.region_3.4_spmd.clone, body=%wide.region_2.3_spmd.clone.sunk | while | flops 65540 | bytes 196905 | solution.py:31
  138.3 49.6 %all-reduce.2 = bf16[256,256]{1,0:T(8,128)(2,1)} all-reduce(f32[256,256]{1,0:T(8,128)S(1)} %convolution_add_fusion), channel_id=1, replica_groups=mesh['ctx'=32,'tp'=16] {'tp'}, use_global_device_ids=true, to_apply=%region_5.6 | all-reduce | flops 65536 | bytes 393216 | tf_op jit(solution)/shard_map/psum | solution.py:104
  189.8 81.9 %all-gather.5.cloned.1.call-done = bf16[8192,256]{1,0:T(8,128)(2,1)} async-done(((bf16[256,256]{1,0:T(8,128)(2,1)}), bf16[8192,256]{1,0:T(8,128)(2,1)}) %all-gather.5.cloned.1.call-update) | async-done | bytes 4194320 | tf_op jit(solution)/shard_map/all_gather | solution.py:161
  271.7 86.4 %while.37 = (s32[]{:T(128)}, f32[1,4,256]{2,1,0:T(4,128)S(1)}, f32[1,4,256]{2,1,0:T(4,128)S(1)}, f32[1,4,256,128]{3,2,1,0:T(8,128)S(1)}, s32[]{:T(128)}, /*index...) while((s32[]{:T(128)}, f32[1,4,256]{2,1,0:T(4,128)S(1)}, ...), condition=%wide.region_13.14_spmd.clone, body=%wide.region_6.13_spmd.clone.sunk | while | flops 339742464 | bytes 9118155 | solution.py:183
  272.3 4.7 %conditional.4 = ((f32[1,4,256]{2,1,0:T(4,128)S(1)}, f32[1,4,256]{2,1,0:T(4,128)S(1)}, f32[1,4,256,128]{3,2,1,0:T(8,128)S(1)})) conditional(s32[]{:T(128)} %convert_element_type.95, (f32[1,4,256]{2,1,0:T(4,128)S(1)}, f32[1,4,256]{2,1,0:T(4,128)S(1)}, f32[1,4,256,128]{3,2,1,0:T(8,128)S(1)}) %tuple.89, (s32[]{:T(128)}, s32[]{:T(128)}, s32[]{:T(128)}, ...), branch_computations={%region_7.7_spmd, %region_8.12_spmd} | conditional | flops 339742464 | bytes 9116868 | solution.py:181
  277.7 4.8 %conditional.4 = ((f32[1,4,256]{2,1,0:T(4,128)S(1)}, f32[1,4,256]{2,1,0:T(4,128)S(1)}, f32[1,4,256,128]{3,2,1,0:T(8,128)S(1)})) conditional(s32[]{:T(128)} %convert_element_type.95, (f32[1,4,256]{2,1,0:T(4,128)S(1)}, f32[1,4,256]{2,1,0:T(4,128)S(1)}, f32[1,4,256,128]{3,2,1,0:T(8,128)S(1)}) %tuple.89, (s32[]{:T(128)}, s32[]{:T(128)}, s32[]{:T(128)}, ...), branch_computations={%region_7.7_spmd, %region_8.12_spmd} | conditional | flops 339742464 | bytes 9116868 | solution.py:181
  283.1 4.7 %conditional.4 = ((f32[1,4,256]{2,1,0:T(4,128)S(1)}, f32[1,4,256]{2,1,0:T(4,128)S(1)}, f32[1,4,256,128]{3,2,1,0:T(8,128)S(1)})) conditional(s32[]{:T(128)} %convert_element_type.95, (f32[1,4,256]{2,1,0:T(4,128)S(1)}, f32[1,4,256]{2,1,0:T(4,128)S(1)}, f32[1,4,256,128]{3,2,1,0:T(8,128)S(1)}) %tuple.89, (s32[]{:T(128)}, s32[]{:T(128)}, s32[]{:T(128)}, ...), branch_computations={%region_7.7_spmd, %region_8.12_spmd} | conditional | flops 339742464 | bytes 9116868 | solution.py:181
  288.5 4.8 %conditional.4 = ((f32[1,4,256]{2,1,0:T(4,128)S(1)}, f32[1,4,256]{2,1,0:T(4,128)S(1)}, f32[1,4,256,128]{3,2,1,0:T(8,128)S(1)})) conditional(s32[]{:T(128)} %convert_element_type.95, (f32[1,4,256]{2,1,0:T(4,128)S(1)}, f32[1,4,256]{2,1,0:T(4,128)S(1)}, f32[1,4,256,128]{3,2,1,0:T(8,128)S(1)}) %tuple.89, (s32[]{:T(128)}, s32[]{:T(128)}, s32[]{:T(128)}, ...), branch_computations={%region_7.7_spmd, %region_8.12_spmd} | conditional | flops 339742464 | bytes 9116868 | solution.py:181
  293.9 4.7 %conditional.4 = ((f32[1,4,256]{2,1,0:T(4,128)S(1)}, f32[1,4,256]{2,1,0:T(4,128)S(1)}, f32[1,4,256,128]{3,2,1,0:T(8,128)S(1)})) conditional(s32[]{:T(128)} %convert_element_type.95, (f32[1,4,256]{2,1,0:T(4,128)S(1)}, f32[1,4,256]{2,1,0:T(4,128)S(1)}, f32[1,4,256,128]{3,2,1,0:T(8,128)S(1)}) %tuple.89, (s32[]{:T(128)}, s32[]{:T(128)}, s32[]{:T(128)}, ...), branch_computations={%region_7.7_spmd, %region_8.12_spmd} | conditional | flops 339742464 | bytes 9116868 | solution.py:181
  299.3 4.8 %conditional.4 = ((f32[1,4,256]{2,1,0:T(4,128)S(1)}, f32[1,4,256]{2,1,0:T(4,128)S(1)}, f32[1,4,256,128]{3,2,1,0:T(8,128)S(1)})) conditional(s32[]{:T(128)} %convert_element_type.95, (f32[1,4,256]{2,1,0:T(4,128)S(1)}, f32[1,4,256]{2,1,0:T(4,128)S(1)}, f32[1,4,256,128]{3,2,1,0:T(8,128)S(1)}) %tuple.89, (s32[]{:T(128)}, s32[]{:T(128)}, s32[]{:T(128)}, ...), branch_computations={%region_7.7_spmd, %region_8.12_spmd} | conditional | flops 339742464 | bytes 9116868 | solution.py:181
  302.3 1.7 conditional
  304.7 4.7 %conditional.4 = ((f32[1,4,256]{2,1,0:T(4,128)S(1)}, f32[1,4,256]{2,1,0:T(4,128)S(1)}, f32[1,4,256,128]{3,2,1,0:T(8,128)S(1)})) conditional(s32[]{:T(128)} %convert_element_type.95, (f32[1,4,256]{2,1,0:T(4,128)S(1)}, f32[1,4,256]{2,1,0:T(4,128)S(1)}, f32[1,4,256,128]{3,2,1,0:T(8,128)S(1)}) %tuple.89, (s32[]{:T(128)}, s32[]{:T(128)}, s32[]{:T(128)}, ...), branch_computations={%region_7.7_spmd, %region_8.12_spmd} | conditional | flops 339742464 | bytes 9116868 | solution.py:181
  310.1 4.8 %conditional.4 = ((f32[1,4,256]{2,1,0:T(4,128)S(1)}, f32[1,4,256]{2,1,0:T(4,128)S(1)}, f32[1,4,256,128]{3,2,1,0:T(8,128)S(1)})) conditional(s32[]{:T(128)} %convert_element_type.95, (f32[1,4,256]{2,1,0:T(4,128)S(1)}, f32[1,4,256]{2,1,0:T(4,128)S(1)}, f32[1,4,256,128]{3,2,1,0:T(8,128)S(1)}) %tuple.89, (s32[]{:T(128)}, s32[]{:T(128)}, s32[]{:T(128)}, ...), branch_computations={%region_7.7_spmd, %region_8.12_spmd} | conditional | flops 339742464 | bytes 9116868 | solution.py:181
  315.5 4.7 %conditional.4 = ((f32[1,4,256]{2,1,0:T(4,128)S(1)}, f32[1,4,256]{2,1,0:T(4,128)S(1)}, f32[1,4,256,128]{3,2,1,0:T(8,128)S(1)})) conditional(s32[]{:T(128)} %convert_element_type.95, (f32[1,4,256]{2,1,0:T(4,128)S(1)}, f32[1,4,256]{2,1,0:T(4,128)S(1)}, f32[1,4,256,128]{3,2,1,0:T(8,128)S(1)}) %tuple.89, (s32[]{:T(128)}, s32[]{:T(128)}, s32[]{:T(128)}, ...), branch_computations={%region_7.7_spmd, %region_8.12_spmd} | conditional | flops 339742464 | bytes 9116868 | solution.py:181
  320.9 4.8 %conditional.4 = ((f32[1,4,256]{2,1,0:T(4,128)S(1)}, f32[1,4,256]{2,1,0:T(4,128)S(1)}, f32[1,4,256,128]{3,2,1,0:T(8,128)S(1)})) conditional(s32[]{:T(128)} %convert_element_type.95, (f32[1,4,256]{2,1,0:T(4,128)S(1)}, f32[1,4,256]{2,1,0:T(4,128)S(1)}, f32[1,4,256,128]{3,2,1,0:T(8,128)S(1)}) %tuple.89, (s32[]{:T(128)}, s32[]{:T(128)}, s32[]{:T(128)}, ...), branch_computations={%region_7.7_spmd, %region_8.12_spmd} | conditional | flops 339742464 | bytes 9116868 | solution.py:181
  323.9 1.7 conditional
  326.3 4.7 %conditional.4 = ((f32[1,4,256]{2,1,0:T(4,128)S(1)}, f32[1,4,256]{2,1,0:T(4,128)S(1)}, f32[1,4,256,128]{3,2,1,0:T(8,128)S(1)})) conditional(s32[]{:T(128)} %convert_element_type.95, (f32[1,4,256]{2,1,0:T(4,128)S(1)}, f32[1,4,256]{2,1,0:T(4,128)S(1)}, f32[1,4,256,128]{3,2,1,0:T(8,128)S(1)}) %tuple.89, (s32[]{:T(128)}, s32[]{:T(128)}, s32[]{:T(128)}, ...), branch_computations={%region_7.7_spmd, %region_8.12_spmd} | conditional | flops 339742464 | bytes 9116868 | solution.py:181
  331.7 4.8 %conditional.4 = ((f32[1,4,256]{2,1,0:T(4,128)S(1)}, f32[1,4,256]{2,1,0:T(4,128)S(1)}, f32[1,4,256,128]{3,2,1,0:T(8,128)S(1)})) conditional(s32[]{:T(128)} %convert_element_type.95, (f32[1,4,256]{2,1,0:T(4,128)S(1)}, f32[1,4,256]{2,1,0:T(4,128)S(1)}, f32[1,4,256,128]{3,2,1,0:T(8,128)S(1)}) %tuple.89, (s32[]{:T(128)}, s32[]{:T(128)}, s32[]{:T(128)}, ...), branch_computations={%region_7.7_spmd, %region_8.12_spmd} | conditional | flops 339742464 | bytes 9116868 | solution.py:181
  337.1 4.7 %conditional.4 = ((f32[1,4,256]{2,1,0:T(4,128)S(1)}, f32[1,4,256]{2,1,0:T(4,128)S(1)}, f32[1,4,256,128]{3,2,1,0:T(8,128)S(1)})) conditional(s32[]{:T(128)} %convert_element_type.95, (f32[1,4,256]{2,1,0:T(4,128)S(1)}, f32[1,4,256]{2,1,0:T(4,128)S(1)}, f32[1,4,256,128]{3,2,1,0:T(8,128)S(1)}) %tuple.89, (s32[]{:T(128)}, s32[]{:T(128)}, s32[]{:T(128)}, ...), branch_computations={%region_7.7_spmd, %region_8.12_spmd} | conditional | flops 339742464 | bytes 9116868 | solution.py:181
  342.5 4.8 %conditional.4 = ((f32[1,4,256]{2,1,0:T(4,128)S(1)}, f32[1,4,256]{2,1,0:T(4,128)S(1)}, f32[1,4,256,128]{3,2,1,0:T(8,128)S(1)})) conditional(s32[]{:T(128)} %convert_element_type.95, (f32[1,4,256]{2,1,0:T(4,128)S(1)}, f32[1,4,256]{2,1,0:T(4,128)S(1)}, f32[1,4,256,128]{3,2,1,0:T(8,128)S(1)}) %tuple.89, (s32[]{:T(128)}, s32[]{:T(128)}, s32[]{:T(128)}, ...), branch_computations={%region_7.7_spmd, %region_8.12_spmd} | conditional | flops 339742464 | bytes 9116868 | solution.py:181
  347.9 4.7 %conditional.4 = ((f32[1,4,256]{2,1,0:T(4,128)S(1)}, f32[1,4,256]{2,1,0:T(4,128)S(1)}, f32[1,4,256,128]{3,2,1,0:T(8,128)S(1)})) conditional(s32[]{:T(128)} %convert_element_type.95, (f32[1,4,256]{2,1,0:T(4,128)S(1)}, f32[1,4,256]{2,1,0:T(4,128)S(1)}, f32[1,4,256,128]{3,2,1,0:T(8,128)S(1)}) %tuple.89, (s32[]{:T(128)}, s32[]{:T(128)}, s32[]{:T(128)}, ...), branch_computations={%region_7.7_spmd, %region_8.12_spmd} | conditional | flops 339742464 | bytes 9116868 | solution.py:181
  353.3 4.8 %conditional.4 = ((f32[1,4,256]{2,1,0:T(4,128)S(1)}, f32[1,4,256]{2,1,0:T(4,128)S(1)}, f32[1,4,256,128]{3,2,1,0:T(8,128)S(1)})) conditional(s32[]{:T(128)} %convert_element_type.95, (f32[1,4,256]{2,1,0:T(4,128)S(1)}, f32[1,4,256]{2,1,0:T(4,128)S(1)}, f32[1,4,256,128]{3,2,1,0:T(8,128)S(1)}) %tuple.89, (s32[]{:T(128)}, s32[]{:T(128)}, s32[]{:T(128)}, ...), branch_computations={%region_7.7_spmd, %region_8.12_spmd} | conditional | flops 339742464 | bytes 9116868 | solution.py:181
  (338 shorter events, 133.7 us)
Async XLA Ops:
  7.2 130.5 %copy-start = (bf16[1024,256]{1,0:T(8,128)(2,1)S(1)}, bf16[1024,256]{1,0:T(8,128)(2,1)}, u32[]{:S(2)}) copy-start(bf16[1024,256]{1,0:T(8,128)(2,1)} %param.29) | copy-start | bytes 1572868
  7.2 4.4 %copy-start.5 = (bf16[16,256]{1,0:T(8,128)(2,1)S(1)}, bf16[16,256]{1,0:T(8,128)(2,1)}, u32[]{:S(2)}) copy-start(bf16[16,256]{1,0:T(8,128)(2,1)} %param.25) | copy-start | bytes 24580
  7.2 95.1 %all-gather.7.cloned.1.call-start = ((), (), s32[]{:S(2)}) async-start(), calls=%async_computation.1 | async-start | bytes 4325376 | tf_op jit(solution)/shard_map/all_gather | solution.py:22
  10.2 75.7 %copy-start.6 = (bf16[16,256]{1,0:T(8,128)(2,1)S(1)}, bf16[16,256]{1,0:T(8,128)(2,1)}, u32[]{:S(2)}) copy-start(bf16[16,256]{1,0:T(8,128)(2,1)} %param.26) | copy-start | bytes 24580
  13.0 122.5 %copy-start.8 = (f32[16]{0:T(128)S(1)}, f32[16]{0:T(128)}, u32[]{:S(2)}) copy-start(f32[16]{0:T(128)} %param.27) | copy-start | bytes 196
  13.0 258.6 %all-gather.5.cloned.1.call-start = ((), (), s32[]{:S(2)}) async-start(), calls=%async_computation | async-start | bytes 4325376 | tf_op jit(solution)/shard_map/all_gather | solution.py:161
  136.9 0.7 copy-start.7
  137.0 1.0 copy-start.3
  137.0 1.0 copy-start.4
  137.6 51.0 %copy-start.2 = (bf16[256,512]{1,0:T(8,128)(2,1)S(1)}, bf16[256,512]{1,0:T(8,128)(2,1)}, u32[]{:S(2)}) copy-start(bf16[256,512]{1,0:T(8,128)(2,1)} %param.33) | copy-start | bytes 786436
  137.7 52.1 %copy-start.1 = (bf16[256,1024]{1,0:T(8,128)(2,1)}, bf16[256,1024]{1,0:T(8,128)(2,1)S(1)}, u32[]{:S(2)}) copy-start(bf16[256,1024]{1,0:T(8,128)(2,1)S(1)} %multiply_convert_fusion.8) | copy-start | bytes 1572868
Sparse Core Ops, SparseCore 0:
  13.1 89.1 all-gather.6
  188.0 83.5 all-gather.4
where the time goes:
time: 368 us; the launch traced here: 366 us
  blocking collectives  120 us (33%)
  waiting for transfers between devices  98 us (27%)
  matrix products  61 us (17%)
  other arithmetic  41.6 us (11%)
  loops' own time  23.1 us (6%)
  between operations  15.1 us (4%)
  local copies, waits for them, and re-layouts  7.03 us (2%)
    all_gather x1, waiting for transfers between devices, body(): portion = lax.all_gather(latents, 'ctx', axis=0, tiled=True)  81.9 us
    unnamed x1, blocking collectives  70.6 us
    psum x1, blocking collectives, body(): latents = lax.psum(latent_terms, 'tp').astype(jnp.bfloat16)  49.6 us
    select_n x31, other arithmetic, lap(): jnp.where(position < mine, new, old)  30.9 us
    dot_general x16, matrix products, from_latents(): jnp.dot(latent_blk, value_columns, preferred_element_type=jnp.float32)  18.8 us
    dot_general x16, matrix products, from_latents(): jnp.dot(latent_blk, key_columns, preferred_element_type=jnp.float32)  18.8 us
    all_gather x1, waiting for transfers between devices, carried_in(): pieces = jax.tree.map(lambda part: lax.all_gather(part, axis), value)  16.2 us
    dot_general x16, matrix products, absorb(): jnp.einsum('kgts,skd->kgtd', weights.astype(jnp.bfloat16), value_blk, pre...  11.5 us
  transfers between devices with their start and end apart: 2, of which 2 were waited for; matrix products, arithmetic and copies ran while one was open for 1% of the time, Pallas kernels for 0%

commit v1 on v0

v1 whole, which is shorter than its diff:
```python
import functools
import math

import jax
import jax.numpy as jnp
from jax import lax
from jax.experimental import pallas as pl
from jax.experimental.pallas import tpu as pltpu
from jax.sharding import Mesh
from jax.sharding import PartitionSpec as P

STATE = 16
HEADDIM = 64
ROWS = 256
HEADS_SSM = 16
INNER = HEADS_SSM * HEADDIM
HD = 128
RANK = 256
HEADS_Q = 4
NY, NX, NZ, NC = 8, 4, 8, 2
NT = NZ * NC
PIECE = ROWS // NT
HALF = ROWS // NC
NCTX = NY * NX
PAY = INNER + 128
BLOCKS = INNER // 128

NEG_BIG = -1e30
EPSILON = 1e-05
SCALE2 = math.log2(math.e) / math.sqrt(HD)
F32 = jnp.float32
BF16 = jnp.bfloat16
MIB = 1 << 20

VM = pl.BlockSpec(memory_space=pltpu.VMEM)
ANY = pl.BlockSpec(memory_space=pl.ANY)
SM = pl.BlockSpec(memory_space=pltpu.SMEM)


def iota(shape, axis):
    return lax.broadcasted_iota(jnp.int32, shape, axis)


def dot(a, b):
    return jnp.dot(a, b, preferred_element_type=F32)


def split(value):
    high = value.astype(BF16)
    return high, (value - high.astype(F32)).astype(BF16)


def spread():
    lane = iota((128, INNER), 0)
    head = iota((128, INNER), 1) // HEADDIM
    return jnp.where((lane < 2 * HEADS_SSM) & ((lane & 15) == head), 1.0, 0.0).astype(BF16)


def within_rows(step_ref, rate_ref):
    row = iota((HEADS_SSM, ROWS), 0)
    lane = iota((HEADS_SSM, ROWS), 1)
    rate = jnp.zeros((HEADS_SSM, ROWS), F32)
    for h in range(HEADS_SSM):
        rate = jnp.where(row == h, rate_ref[h], rate)
    total = -rate * step_ref[...]
    shift = 1
    while shift < ROWS:
        total = total + jnp.where(lane >= shift, pltpu.roll(total, shift, 1), 0.0)
        shift *= 2
    return total


def pack_decay(compact):
    lane = iota(compact.shape, 1)
    kept = jnp.where(lane < HEADS_SSM, compact, 0.0)
    high = kept.astype(BF16).astype(F32)
    low = pltpu.roll(kept - high, HEADS_SSM, 1)
    return (high + low).astype(BF16)


def unpack_decay(packed):
    value = packed.astype(F32)
    lane = iota(value.shape, 1)
    return jnp.where(lane < HEADS_SSM, value + pltpu.roll(value, 128 - HEADS_SSM, 1), 0.0)


def state_kernel(rate_ref, x_ref, step_ref, b_ref, pay_ref):
    within = within_rows(step_ref, rate_ref)
    last = within[:, ROWS - 1 : ROWS]
    to_end = jnp.exp(last - within)
    b = b_ref[...].astype(F32)
    lane = iota((STATE, 128), 1)
    for j in range(BLOCKS):
        cols = slice(128 * j, 128 * (j + 1))
        a0h, a0l = split(to_end[2 * j : 2 * j + 1, :] * b)
        a1h, a1l = split(to_end[2 * j + 1 : 2 * j + 2, :] * b)
        lhs = jnp.concatenate([a0h, a1h, a0l, a1l], axis=0)
        out = dot(lhs, x_ref[:, cols])
        both = out[: 2 * STATE] + out[2 * STATE :]
        state = jnp.where(lane < HEADDIM, both[:STATE], both[STATE:])
        for i in range(NX):
            pay_ref[i, :, cols] = state.astype(BF16)
    head = iota((HEADS_SSM, 128), 0)
    hlane = iota((HEADS_SSM, 128), 1)
    compact = jnp.sum(jnp.where(hlane == head, jnp.exp(last), 0.0), axis=0, keepdims=True)
    packed = pack_decay(jnp.broadcast_to(compact, (STATE, 128)))
    for i in range(NX):
        pay_ref[i, :, INNER:] = packed


def widened(spans_ref, count):
    packed = jnp.concatenate([spans_ref[i, :, INNER:] for i in range(count)], axis=0)
    wide = dot(packed, spread())
    return [wide[i * STATE : (i + 1) * STATE] for i in range(count)]


def row_kernel(place_ref, spans_ref, total_ref, before_ref, decay_ref):
    x = place_ref[1]
    wide = widened(spans_ref, NX)
    run = jnp.zeros((STATE, INNER), F32)
    before = run
    before_decay = jnp.ones((STATE, INNER), F32)
    compact = jnp.ones((STATE, 128), F32)
    for i in range(NX):
        run = wide[i] * run + spans_ref[i, :, :INNER].astype(F32)
        before = jnp.where(i < x, run, before)
        before_decay = jnp.where(i < x, wide[i] * before_decay, before_decay)
        compact = compact * unpack_decay(spans_ref[i, :, INNER:])
    before_ref[...] = before
    decay_ref[...] = before_decay
    total = run.astype(BF16)
    packed = pack_decay(compact)
    for i in range(NY):
        total_ref[i, :, :INNER] = total
        total_ref[i, :, INNER:] = packed


def intra_kernel(
    rate_ref, skip_ref, x_ref, step_ref, b_ref, c_ref, y_ref, grow_ref
):
    within = within_rows(step_ref, rate_ref)
    columns = jnp.concatenate([within, jnp.zeros((128 - HEADS_SSM, ROWS), F32)], axis=0).T
    grow = jnp.exp(columns)
    grow_ref[...] = pack_decay(grow)
    meet = lax.dot_general(
        c_ref[...], b_ref[...], (((0,), (0,)), ((), ())), preferred_element_type=F32
    )
    half = ROWS // 2
    causal = iota((half, half), 0) >= iota((half, half), 1)
    lane = iota((ROWS, 128), 1)
    zeros = jnp.zeros((half, half), BF16)

    def mixing(h):
        row = within[h : h + 1, :]
        column = columns[:, h : h + 1]
        top, bottom = column[:half], column[half:]
        left, right = row[:, :half], row[:, half:]
        m00 = meet[:half, :half] * jnp.exp(jnp.where(causal, top - left, NEG_BIG))
        m10 = meet[half:, :half] * jnp.exp(bottom - left)
        m11 = meet[half:, half:] * jnp.exp(jnp.where(causal, bottom - right, NEG_BIG))
        upper = jnp.concatenate([m00.astype(BF16), zeros], axis=1)
        lower = jnp.concatenate([m10.astype(BF16), m11.astype(BF16)], axis=1)
        return jnp.concatenate([upper, lower], axis=0)

    for j in range(HEADS_SSM // 2):
        cols = slice(128 * j, 128 * (j + 1))
        x = x_ref[:, cols]
        out0 = dot(mixing(2 * j), x)
        out1 = dot(mixing(2 * j + 1), x)
        skip = jnp.where(lane < HEADDIM, skip_ref[2 * j], skip_ref[2 * j + 1])
        y_ref[:, cols] = jnp.where(lane < HEADDIM, out0, out1) + skip * x.astype(F32)


def finish_kernel(
    place_ref, rows_ref, before_ref, decay_ref, y_ref, grow_ref, c_ref, gain_ref, w_ref, h_ref,
    mamba_ref, part_ref,
):
    chan = spread()
    wide = widened(rows_ref, NY - 1)
    run = jnp.zeros((STATE, INNER), F32)
    for row in range(NY - 1):
        joined = wide[row] * run + rows_ref[row, :, :INNER].astype(F32)
        run = jnp.where(row < place_ref[0], joined, run)
    carried = run * decay_ref[...] + before_ref[...]
    high, low = split(carried)
    c = c_ref[...]
    from_state = lax.dot_general(
        jnp.concatenate([c, c], axis=0),
        jnp.concatenate([high, low], axis=0),
        (((0,), (0,)), ((), ())),
        preferred_element_type=F32,
    )
    grow = dot(grow_ref[...], chan)
    out = y_ref[...] + from_state * grow
    gather = jnp.where(
        iota((INNER, 128), 0) // HEADDIM == iota((INNER, 128), 1), 1.0, 0.0
    ).astype(BF16)
    square = dot((out * out).astype(BF16), gather) * (1.0 / HEADDIM)
    inverse = dot(pack_decay(lax.rsqrt(square + EPSILON)), chan)
    mamba = (out * inverse * gain_ref[...]).astype(BF16)
    mamba_ref[...] = mamba
    part_ref[...] = (dot(mamba, w_ref[...]) + h_ref[...]).astype(BF16)


def copy_kernel(q_ref, out_ref):
    out_ref[...] = q_ref[...]


def sum_kernel(pieces_ref, out_ref):
    total = pieces_ref[0].astype(F32)
    for i in range(1, NT):
        total = total + pieces_ref[i].astype(F32)
    rounded = total.astype(BF16)
    for i in range(NY * NZ):
        out_ref[i] = rounded


def hidden_kernel(hidden_ref, w_ref, out_ref):
    out_ref[...] = dot(hidden_ref[...], w_ref[...])


def weights_kernel(place_ref, wk_ref, wv_ref, order_ref, out_ref):
    out_ref[:, :HD] = wk_ref[...]
    out_ref[:, HD:] = wv_ref[...]


def rebuild_kernel(place_ref, mine_ref, w_ref, out_ref):
    y = place_ref[0]
    w = w_ref[...]
    for block in range(NY):
        begin = ((y - block) & (NY - 1)) * HALF
        out = pl.ds(pl.multiple_of(begin, HALF), HALF)
        rows = dot(mine_ref[block], w)
        out_ref[out, :HD] = (rows[:, :HD] * SCALE2).astype(BF16)
        out_ref[out, HD:] = rows[:, HD:].astype(BF16)


def place_keys(y, mine_ref, other_ref, k_ref, v_ref):
    lane = iota((HALF, HD), 1)
    ones = jnp.ones((HALF, HD), BF16)
    for part, ref in enumerate((mine_ref, other_ref)):
        for block in range(NY):
            rows = slice(block * HALF, (block + 1) * HALF)
            out = slice((part * NY + block) * HALF, (part * NY + block + 1) * HALF)
            bias = jnp.where(y >= block, 0.0, NEG_BIG)
            k_ref[out, :HD] = ref[rows, :HD]
            k_ref[out, HD:] = jnp.where(lane == 0, bias, 0.0).astype(BF16)
            v_ref[out, :HD] = ref[rows, HD:]
            v_ref[out, HD:] = ones


def attend_kernel(step, place_ref, q_ref, k_ref, v_ref, out_ref):
    x, core = place_ref[1], place_ref[3]
    ahead = ((x ^ step) - x) * ROWS
    lane = iota((ROWS, 128), 1)
    unit = jnp.where(lane == 0, 1.0, 0.0).astype(BF16)
    token = iota((ROWS, HALF), 0) + ahead
    slot = iota((ROWS, HALF), 1)
    allowed = []
    for own in (core, 1 - core):
        key = (slot // PIECE) * (2 * PIECE) + own * PIECE + (slot & (PIECE - 1))
        allowed.append(key <= token)

    allowed = [jnp.concatenate([part, part], axis=0) for part in allowed]

    def scored(first, part):
        query = jnp.concatenate(
            [
                jnp.concatenate([q_ref[:, h * HD : (h + 1) * HD], unit], axis=1)
                for h in (first, first + 1)
            ],
            axis=0,
        )
        scores = lax.dot_general(
            query,
            k_ref[part * NY * HALF : (part + 1) * NY * HALF, :],
            (((1,), (1,)), ((), ())),
            preferred_element_type=F32,
        )
        near = jnp.where(allowed[part], scores[:, :HALF], NEG_BIG)
        return jnp.concatenate([near, scores[:, HALF:]], axis=1)

    stats = jnp.zeros((ROWS, 128), F32)
    following = scored(0, 0)
    for first in range(0, HEADS_Q, 2):
        best = sums = None
        for part in range(2):
            scores = following
            if part == 0:
                following = scored(first, 1)
            elif first + 2 < HEADS_Q:
                following = scored(first + 2, 0)
            chunk_best = jnp.max(scores, axis=1, keepdims=True)
            values = v_ref[part * NY * HALF : (part + 1) * NY * HALF, :]
            if part == 0:
                best = chunk_best
                sums = dot(jnp.exp2(scores - best).astype(BF16), values)
            else:
                old, best = best, jnp.maximum(best, chunk_best)
                sums = sums * jnp.exp2(old - best) + dot(
                    jnp.exp2(scores - best).astype(BF16), values
                )
        norm = sums[:, HD:]
        ratio = (sums[:, :HD] / norm).astype(BF16)
        level = best + jnp.log2(norm)
        for h in (first, first + 1):
            rows = slice((h - first) * ROWS, (h - first + 1) * ROWS)
            out_ref[:ROWS, h * HD : (h + 1) * HD] = ratio[rows]
            stats = jnp.where(lane == h, level[rows], stats)
    rows = stats.T[:8, :]
    high, mid = split(rows)
    low = (rows - high.astype(F32) - mid.astype(F32)).astype(BF16)
    upper = jnp.concatenate([high, mid], axis=1)
    lower = jnp.concatenate([low, jnp.zeros((8, ROWS), BF16)], axis=1)
    out_ref[ROWS:, :] = jnp.concatenate([upper, lower], axis=0)


def attend_first_kernel(step, place_ref, q_ref, mine_ref, other_ref, out_ref, k_ref, v_ref):
    place_keys(place_ref[0], mine_ref, other_ref, k_ref, v_ref)
    attend_kernel(step, place_ref, q_ref, k_ref, v_ref, out_ref)


def combine_kernel(own_ref, back1_ref, back2_ref, back3_ref, out_ref):
    refs = [own_ref, back1_ref, back2_ref, back3_ref]
    logs = []
    for ref in refs:
        tail = ref[ROWS:, :].astype(F32)
        logs.append(tail[:8, :ROWS] + tail[:8, ROWS:] + tail[8:, :ROWS])
    best = jnp.maximum(jnp.maximum(logs[0], logs[1]), jnp.maximum(logs[2], logs[3]))
    shares = [jnp.exp2(log - best) for log in logs]
    inverse = 1.0 / (shares[0] + shares[1] + shares[2] + shares[3])
    table = jnp.concatenate(
        [share * inverse for share in shares] + [jnp.zeros((128 - 32, ROWS), F32)], axis=0
    ).T
    for h in range(HEADS_Q):
        cols = slice(h * HD, (h + 1) * HD)
        total = jnp.zeros((ROWS, HD), F32)
        for i, ref in enumerate(refs):
            total += table[:, 8 * i + h : 8 * i + h + 1] * ref[:ROWS, cols].astype(F32)
        out_ref[:, cols] = total.astype(BF16)


def call(kernel, name, out_shape, in_specs, limit, flops, moved, streamed=False, **options):
    out_specs = jax.tree.map(lambda _: VM, out_shape)
    if streamed:
        options["grid"] = (1,)
        in_specs = [
            spec if spec in (SM, ANY) else pl.BlockSpec(spec, lambda i, n=len(spec): (0,) * n)
            for spec in in_specs
        ]
        out_specs = jax.tree.map(
            lambda out: pl.BlockSpec(out.shape, lambda i, n=len(out.shape): (0,) * n), out_shape
        )
    return pl.pallas_call(
        kernel,
        out_shape=out_shape,
        in_specs=in_specs,
        out_specs=out_specs,
        name=name,
        cost_estimate=pl.CostEstimate(flops=flops, bytes_accessed=moved, transcendentals=0),
        compiler_params=pltpu.CompilerParams(vmem_limit_bytes=limit * MIB),
        **options,
    )


def shape(dims, kind):
    return jax.ShapeDtypeStruct(dims, kind)


def swap(value, axis, size, step):
    return lax.ppermute(value, axis, [(i, i ^ step) for i in range(size)])


def exchange(chunks, axes):
    return lax.all_to_all(chunks, axes, 0, 0, tiled=True)


def after(kernel, inputs):
    def ordered(*refs):
        kernel(*refs[:inputs], *refs[inputs + 1 :])

    return ordered


def body(
    hidden_states,
    ssm_input,
    step_size,
    decay_rate,
    proj_b,
    proj_c,
    skip_gain,
    norm_gain,
    latent_from_ssm,
    latent_from_hidden,
    key_rebuild,
    value_rebuild,
    queries,
):
    place = jnp.stack(
        [lax.axis_index(axis) for axis in ("y", "x", "z", "core")]
    ).astype(jnp.int32)

    payload = call(
        state_kernel,
        "state",
        shape((NX, STATE, PAY), BF16),
        [SM, (ROWS, INNER), (HEADS_SSM, ROWS), (STATE, ROWS)],
        60,
        1 << 27,
        MIB,
        streamed=True,
    )(decay_rate, ssm_input, step_size, proj_b)
    spans = exchange(payload, "x")
    from_hidden = call(
        after(hidden_kernel, 2),
        "hidden",
        shape((ROWS, RANK), F32),
        [VM, VM, ANY],
        16,
        1 << 31,
        MIB,
    )(hidden_states, latent_from_hidden, payload)
    totals, before, row_decay = call(
        after(row_kernel, 2),
        "row",
        (
            shape((NY, STATE, PAY), BF16),
            shape((STATE, INNER), F32),
            shape((STATE, INNER), F32),
        ),
        [SM, VM, ANY],
        8,
        1 << 24,
        MIB // 2,
    )(place, spans, from_hidden)

    rows = exchange(totals, "y")
    partial, growth = call(
        after(intra_kernel, 6),
        "intra",
        (shape((ROWS, INNER), F32), shape((ROWS, 128), BF16)),
        [SM, SM] + [VM] * 4 + [ANY],
        24,
        1 << 31,
        3 * MIB,
    )(decay_rate, skip_gain, ssm_input, step_size, proj_b, proj_c, before)
    mamba_out, latent_terms = call(
        finish_kernel,
        "finish",
        (shape((ROWS, INNER), BF16), shape((ROWS, RANK), BF16)),
        [SM] + [VM] * 9,
        24,
        1 << 29,
        4 * MIB,
    )(
        place, rows, before, row_decay, partial, growth, proj_c, norm_gain.reshape(1, INNER),
        latent_from_ssm, from_hidden,
    )

    def copied(done):
        return call(
            after(copy_kernel, 1), "copy", shape(queries.shape, BF16), [VM, ANY], 8, 1 << 27, MIB
        )(queries, done)

    pieces = exchange(latent_terms.reshape(NT, PIECE, RANK), ("z", "core"))
    lent = copied(latent_terms)
    latents = call(
        after(sum_kernel, 1),
        "sum",
        shape((NY * NZ, PIECE, RANK), BF16),
        [VM, ANY],
        8,
        1 << 20,
        MIB // 2,
    )(pieces, lent)

    blocks = exchange(latents, ("y", "z")).reshape(NY, HALF, RANK)
    lent = copied(latents)
    visiting1, visiting2, visiting3 = [swap(lent, "x", NX, k) for k in (1, 2, 3)]
    weights = pl.pallas_call(
        weights_kernel,
        out_shape=shape((RANK, 2 * HD), BF16),
        grid_spec=pltpu.PrefetchScalarGridSpec(
            num_scalar_prefetch=1,
            grid=(1,),
            in_specs=[pl.BlockSpec((RANK, HD), lambda i, place: (0, place[2]))] * 2 + [ANY],
            out_specs=pl.BlockSpec((RANK, 2 * HD), lambda i, place: (0, 0)),
        ),
        name="weights",
        cost_estimate=pl.CostEstimate(flops=1 << 30, bytes_accessed=MIB, transcendentals=0),
        compiler_params=pltpu.CompilerParams(vmem_limit_bytes=8 * MIB),
    )(place, key_rebuild, value_rebuild, latents)
    mine = call(
        after(after(after(rebuild_kernel, 3), 3), 3),
        "rebuild",
        shape((NY * HALF, 2 * HD), BF16),
        [SM, VM, VM, ANY, ANY, ANY],
        8,
        1 << 27,
        MIB,
    )(place, blocks, weights, visiting1, visiting2, visiting3)
    other = swap(mine, "core", NC, 1)

    work = 4 * ROWS * HEADS_Q * HD * NY * ROWS
    answer = shape((ROWS + 16, HEADS_Q * HD), BF16)
    wide = shape((NY * ROWS, 2 * HD), BF16)
    done, keys, values = call(
        functools.partial(attend_first_kernel, 2), "attend", (answer, wide, wide),
        [SM, VM, VM, VM], 24, work, 4 * MIB,
    )(place, visiting2, mine, other)
    back = {2: swap(done, "x", NX, 2)}
    for step, query, awaited in ((1, visiting1, None), (3, visiting3, None), (0, queries, 2)):
        kernel = functools.partial(attend_kernel, step)
        operands = [place, query, keys, values, done]
        if awaited is not None:
            operands.append(back[awaited])
            kernel = after(kernel, 4)
        done = call(
            after(kernel, 4), "attend", answer, [SM, VM, VM, VM] + [ANY] * (len(operands) - 4),
            24, work, 4 * MIB,
        )(*operands)
        if step:
            back[step] = swap(done, "x", NX, step)

    attended = call(
        combine_kernel,
        "combine",
        shape((ROWS, HEADS_Q * HD), BF16),
        [VM] * 4,
        16,
        1 << 20,
        2 * MIB,
    )(done, back[1], back[2], back[3])
    return (mamba_out, attended)


def solution(mesh):
    grid = Mesh(mesh.devices.reshape(NY, NX, NZ, NC), ("y", "x", "z", "core"))
    ctx, tp = ("y", "x"), ("z", "core")
    return jax.shard_map(
        body,
        mesh=grid,
        in_specs=(
            P(ctx, tp),
            P(ctx, tp),
            P(tp, ctx),
            P(tp),
            P(None, ctx),
            P(None, ctx),
            P(tp),
            P(tp),
            P(tp, None),
            P(tp, None),
            P(),
            P(),
            P(ctx, tp),
        ),
        out_specs=(P(ctx, tp), P(ctx, tp)),
        check_vma=False,
    )
```

time: 368 us -> 116 us (0.32)
  the two profiles are of different devices: /device:TPU:60 before, /device:TPU:16 now
where the time goes in v1:
time: 116 us; the launch traced here: 115 us
  starting transfers between devices  51.3 us (44%)
  waiting for transfers between devices  35.8 us (31%)
  Pallas kernels  26.3 us (23%)
    all_to_all x4, starting transfers between devices, exchange(): return lax.all_to_all(chunks, axes, 0, 0, tiled=True)  29.4 us
    ppermute x7, starting transfers between devices, swap(): return lax.ppermute(value, axis, [(i, i ^ step) for i in range(size)])  21.9 us
    all_to_all x4, waiting for transfers between devices, exchange(): return lax.all_to_all(chunks, axes, 0, 0, tiled=True)  19.9 us
    ppermute x7, waiting for transfers between devices, swap(): return lax.ppermute(value, axis, [(i, i ^ step) for i in range(size)])  15.9 us
    pallas_call x3, Pallas kernels, body(): call(after(kernel, 4), 'attend', answer, [SM, VM, VM, VM] + [ANY] * (len(...  9.82 us
    pallas_call x1, Pallas kernels, body(): call(functools.partial(attend_first_kernel, 2), 'attend', (answer, wide,...  3.58 us
    pallas_call x1, Pallas kernels, body(): call(finish_kernel, 'finish', (shape((ROWS, INNER), BF16), shape((ROWS, R...  2.61 us
    pallas_call x1, Pallas kernels, body(): call(state_kernel, 'state', shape((NX, STATE, PAY), BF16), [SM, (ROWS, IN...  2.59 us
  transfers between devices with their start and end apart: 11, of which 9 were waited for; matrix products, arithmetic and copies ran while one was open for 0% of the time, Pallas kernels for 11%

profile of v1, /device:TPU:16, one launch (start us, length us, event | category | flops | bytes accessed | tf_op | source)
XLA Modules:
  0.0 115.1 jit_solution(10517739357176088363)
XLA Ops:
  0.6 2.6 %state.1.refs_2_ = bf16[4,16,1152]{2,1,0:T(8,128)(2,1)} custom-call(f32[16]{0:T(128)} %refs_0_.5, bf16[256,1024]{1,0:T(8,128)(2,1)} %refs_2_.1, f32[16,256]{1,0:T(8,128)} %refs_3_.1, bf16[16,256]{1,0:T(8,128)(2,1)} %refs_4_.1), custom_call_target="tpu_custom_call" | custom-call | flops 134217728 | bytes 1048576 | tf_op jit(solution)/shard_map/state/pallas_call | solution.py:404
  3.2 4.4 %all-to-all-start = ((bf16[4,16,1152]{2,1,0:T(8,128)(2,1)}), bf16[4,16,1152]{2,1,0:T(8,128)(2,1)S(1)}, u32[]{:S(2)}, u32[]{:S(2)}) async-start(bf16[4,16,1152]{2,1,0:T(8,128)(2,1)} %state.1.refs_2_), calls=%async_computation | async-start | bytes 294912 | tf_op jit(solution)/shard_map/all_to_all | solution.py:375
  8.0 5.7 %all-to-all-done.refs_1_ = bf16[4,16,1152]{2,1,0:T(8,128)(2,1)S(1)} async-done(((bf16[4,16,1152]{2,1,0:T(8,128)(2,1)}), bf16[4,16,1152]{2,1,0:T(8,128)(2,1)S(1)}, u32[]{:S(2)}, u32[]{:S(2)}) %all-to-all-start) | async-done | bytes 147488 | tf_op jit(solution)/shard_map/all_to_all | solution.py:375
  15.2 8.2 %all-to-all-start.1 = ((bf16[8,16,1152]{2,1,0:T(8,128)(2,1)}), bf16[8,16,1152]{2,1,0:T(8,128)(2,1)S(1)}, u32[]{:S(2)}, u32[]{:S(2)}) async-start(bf16[8,16,1152]{2,1,0:T(8,128)(2,1)} %get-tuple-element.12), calls=%async_computation.1 | async-start | bytes 589824 | tf_op jit(solution)/shard_map/all_to_all | solution.py:375
  24.0 2.2 %intra.1 = (f32[256,1024]{1,0:T(8,128)S(1)}, bf16[256,128]{1,0:T(8,128)(2,1)S(1)}) custom-call(f32[16]{0:T(128)S(1)} %copy-done.8, f32[16]{0:T(128)S(1)} %copy-done.13, bf16[256,1024]{1,0:T(8,128)(2,1)S(1)} %copy-done.3, f32[16,256]{1,0:T(8,128)S(1)} %copy-done.4, bf16[16,256]{1,0:T(8,128)(2,1)S(1)} %copy-done.5, bf16[16,256]{1,0:T(8,128)(2,1)S(1)} %copy-done.6, ...), custom_call_target="tpu_custom_call" | custom-call | flops 2147483648 | bytes 3145728 | tf_op jit(solution)/shard_map/intra/pallas_call | solution.py:439
  26.3 5.5 %all-to-all-done.1.rows_ref = bf16[8,16,1152]{2,1,0:T(8,128)(2,1)S(1)} async-done(((bf16[8,16,1152]{2,1,0:T(8,128)(2,1)}), bf16[8,16,1152]{2,1,0:T(8,128)(2,1)S(1)}, u32[]{:S(2)}, u32[]{:S(2)}) %all-to-all-start.1) | async-done | bytes 294944 | tf_op jit(solution)/shard_map/all_to_all | solution.py:375
  31.8 2.6 %finish.1 = (bf16[256,1024]{1,0:T(8,128)(2,1)}, bf16[256,256]{1,0:T(8,128)(2,1)}) custom-call(s32[4]{0:T(128)S(1)} %pad_add_fusion.refs_0_.place_ref, bf16[8,16,1152]{2,1,0:T(8,128)(2,1)S(1)} %all-to-all-done.1.rows_ref, f32[16,1024]{1,0:T(8,128)S(1)} %get-tuple-element.13.refs_6_.before_ref, f32[16,1024]{1,0:T(8,128)S(1)} %get-tuple-element.14.decay_ref, ...), custom_call_target="tpu_custom_call" | custom-call | flops 536870912 | bytes 4194304 | tf_op jit(solution)/shard_map/finish/pallas_call | solution.py:448
  34.4 9.9 %all-to-all-start.2 = ((bf16[16,16,256]{2,1,0:T(8,128)(2,1)}), bf16[16,16,256]{2,1,0:T(8,128)(2,1)S(1)}, u32[]{:S(2)}, u32[]{:S(2)}) async-start(bf16[16,16,256]{2,1,0:T(8,128)(2,1)} %bitcast.5), calls=%async_computation.2 | async-start | bytes 262144 | tf_op jit(solution)/shard_map/all_to_all | solution.py:375
  44.4 8.7 %all-to-all-done.2.refs_0_ = bf16[16,16,256]{2,1,0:T(8,128)(2,1)S(1)} async-done(((bf16[16,16,256]{2,1,0:T(8,128)(2,1)}), bf16[16,16,256]{2,1,0:T(8,128)(2,1)S(1)}, u32[]{:S(2)}, u32[]{:S(2)}) %all-to-all-start.2) | async-done | bytes 131104 | tf_op jit(solution)/shard_map/all_to_all | solution.py:375
  54.0 6.9 %all-to-all-start.3 = ((bf16[64,16,256]{2,1,0:T(8,128)(2,1)}), bf16[64,16,256]{2,1,0:T(8,128)(2,1)S(1)}, u32[]{:S(2)}, u32[]{:S(2)}) async-start(bf16[64,16,256]{2,1,0:T(8,128)(2,1)} %sum.1.refs_1_.order_ref), calls=%async_computation.3 | async-start | bytes 1048576 | tf_op jit(solution)/shard_map/all_to_all | solution.py:375
  60.9 3.2 %collective-permute-start.2 = (bf16[256,512]{1,0:T(8,128)(2,1)S(1)}, bf16[256,512]{1,0:T(8,128)(2,1)S(1)}, u32[]{:S(2)}, u32[]{:S(2)}) collective-permute-start(bf16[256,512]{1,0:T(8,128)(2,1)S(1)} %copy.18), channel_id=1, source_target_pairs={{0,48},{16,32},{32,16},{48,0},{1,49},{17,33},{33,17},{49,1},{2,50}... | collective-permute-start | bytes 786440 | tf_op jit(solution)/shard_map/ppermute | solution.py:371
  64.1 1.9 %collective-permute-start.1 = (bf16[256,512]{1,0:T(8,128)(2,1)S(1)}, bf16[256,512]{1,0:T(8,128)(2,1)S(1)}, u32[]{:S(2)}, u32[]{:S(2)}) collective-permute-start(bf16[256,512]{1,0:T(8,128)(2,1)S(1)} %copy.18), channel_id=1, source_target_pairs={{0,16},{16,0},{32,48},{48,32},{1,17},{17,1},{33,49},{49,33},{2,18}... | collective-permute-start | bytes 786440 | tf_op jit(solution)/shard_map/ppermute | solution.py:371
  66.1 5.4 %collective-permute-start = (bf16[256,512]{1,0:T(8,128)(2,1)S(1)}, bf16[256,512]{1,0:T(8,128)(2,1)S(1)}, u32[]{:S(2)}, u32[]{:S(2)}) collective-permute-start(bf16[256,512]{1,0:T(8,128)(2,1)S(1)} %copy.18), channel_id=1, source_target_pairs={{0,32},{16,48},{32,0},{48,16},{1,33},{17,49},{33,1},{49,17},{2,34}... | collective-permute-start | bytes 786440 | tf_op jit(solution)/shard_map/ppermute | solution.py:371
  72.9 2.2 %collective-permute-done.1.refs_3_.refs_1_ = bf16[256,512]{1,0:T(8,128)(2,1)S(1)} collective-permute-done((bf16[256,512]{1,0:T(8,128)(2,1)S(1)}, bf16[256,512]{1,0:T(8,128)(2,1)S(1)}, u32[]{:S(2)}, u32[]{:S(2)}) %collective-permute-start.1) | collective-permute-done | bytes 262176 | tf_op jit(solution)/shard_map/ppermute | solution.py:371
  75.2 6.5 %collective-permute-done.refs_4_.q_ref = bf16[256,512]{1,0:T(8,128)(2,1)S(1)} collective-permute-done((bf16[256,512]{1,0:T(8,128)(2,1)S(1)}, bf16[256,512]{1,0:T(8,128)(2,1)S(1)}, u32[]{:S(2)}, u32[]{:S(2)}) %collective-permute-start) | collective-permute-done | bytes 262176 | tf_op jit(solution)/shard_map/ppermute | solution.py:371
  82.5 1.9 %collective-permute-start.3 = (bf16[1024,256]{1,0:T(8,128)(2,1)S(1)}, bf16[1024,256]{1,0:T(8,128)(2,1)S(1)}, u32[]{:S(2)}, u32[]{:S(2)}) collective-permute-start(bf16[1024,256]{1,0:T(8,128)(2,1)S(1)} %rebuild.1.mine_ref), channel_id=1, source_target_pairs={{0,1},{1,0},{2,3},{3,2},{4,5},{5,4},{6,7},{7,6},{8,9},{9,8},{10,11... | collective-permute-start | bytes 1572872 | tf_op jit(solution)/shard_map/ppermute | solution.py:371
  86.3 3.6 %attend.4 = (bf16[272,512]{1,0:T(8,128)(2,1)S(1)}, bf16[2048,256]{1,0:T(8,128)(2,1)S(1)}, bf16[2048,256]{1,0:T(8,128)(2,1)S(1)}) custom-call(s32[4]{0:T(128)S(1)} %pad_add_fusion.refs_0_.place_ref, bf16[256,512]{1,0:T(8,128)(2,1)S(1)} %collective-permute-done.refs_4_.q_ref, bf16[1024,256]{1,0:T(8,128)(2,1)S(1)} %rebuild.1.mine_ref, ...), custom_call_target="tpu_custom_call" | custom-call | flops 1073741824 | bytes 4194304 | tf_op jit(solution)/shard_map/attend/pallas_call | solution.py:508
  89.9 2.8 %collective-permute-start.4 = (bf16[272,512]{1,0:T(8,128)(2,1)S(1)}, bf16[272,512]{1,0:T(8,128)(2,1)S(1)}, u32[]{:S(2)}, u32[]{:S(2)}) collective-permute-start(bf16[272,512]{1,0:T(8,128)(2,1)S(1)} %get-tuple-element.21.refs_4_), channel_id=1, source_target_pairs={{0,32},{16,48},{32,0},{48,16},{1,33},{17,49},{33,1},{49,17},{2,34}... | collective-permute-start | bytes 835592 | tf_op jit(solution)/shard_map/ppermute | solution.py:371
  92.7 3.3 %attend.5.refs_4_ = bf16[272,512]{1,0:T(8,128)(2,1)S(1)} custom-call(s32[4]{0:T(128)S(1)} %pad_add_fusion.refs_0_.place_ref, bf16[256,512]{1,0:T(8,128)(2,1)S(1)} %collective-permute-done.1.refs_3_.refs_1_, bf16[2048,256]{1,0:T(8,128)(2,1)S(1)} %get-tuple-element.19.refs_2_, bf16[2048,256]{1,0:T(8,128)(2,1)S(1)} %get-tuple-element.20.refs_3_, ...), custom_call_target="tpu_custom_call" | custom-call | flops 1073741824 | bytes 4194304 | tf_op jit(solution)/shard_map/attend/pallas_call | solution.py:519
  95.9 3.3 %attend.6.refs_4_ = bf16[272,512]{1,0:T(8,128)(2,1)S(1)} custom-call(s32[4]{0:T(128)S(1)} %pad_add_fusion.refs_0_.place_ref, bf16[256,512]{1,0:T(8,128)(2,1)S(1)} %collective-permute-done.2.refs_5_.refs_1_, bf16[2048,256]{1,0:T(8,128)(2,1)S(1)} %get-tuple-element.19.refs_2_, bf16[2048,256]{1,0:T(8,128)(2,1)S(1)} %get-tuple-element.20.refs_3_, ...), custom_call_target="tpu_custom_call" | custom-call | flops 1073741824 | bytes 4194304 | tf_op jit(solution)/shard_map/attend/pallas_call | solution.py:519
  99.2 4.4 %collective-permute-start.6 = (bf16[272,512]{1,0:T(8,128)(2,1)S(1)}, bf16[272,512]{1,0:T(8,128)(2,1)S(1)}, u32[]{:S(2)}, u32[]{:S(2)}) collective-permute-start(bf16[272,512]{1,0:T(8,128)(2,1)S(1)} %attend.6.refs_4_), channel_id=1, source_target_pairs={{0,48},{16,32},{32,16},{48,0},{1,49},{17,33},{33,17},{49,1},{2,50}... | collective-permute-start | bytes 835592 | tf_op jit(solution)/shard_map/ppermute | solution.py:371
  103.6 2.3 %collective-permute-start.5 = (bf16[272,512]{1,0:T(8,128)(2,1)S(1)}, bf16[272,512]{1,0:T(8,128)(2,1)S(1)}, u32[]{:S(2)}, u32[]{:S(2)}) collective-permute-start(bf16[272,512]{1,0:T(8,128)(2,1)S(1)} %attend.5.refs_4_), channel_id=1, source_target_pairs={{0,16},{16,0},{32,48},{48,32},{1,17},{17,1},{33,49},{49,33},{2,18}... | collective-permute-start | bytes 835592 | tf_op jit(solution)/shard_map/ppermute | solution.py:371
  105.8 3.3 %attend.7.own_ref = bf16[272,512]{1,0:T(8,128)(2,1)S(1)} custom-call(s32[4]{0:T(128)S(1)} %pad_add_fusion.refs_0_.place_ref, bf16[256,512]{1,0:T(8,128)(2,1)S(1)} %copy-done, bf16[2048,256]{1,0:T(8,128)(2,1)S(1)} %get-tuple-element.19.refs_2_, bf16[2048,256]{1,0:T(8,128)(2,1)S(1)} %get-tuple-element.20.refs_3_, bf16[272,512]{1,0:T(8,128)(2,1)S(1)} %attend.6.refs_4_, ...), custom_call_target="tpu_custom_call" | custom-call | flops 1073741824 | bytes 4194304 | tf_op jit(solution)/shard_map/attend/pallas_call | solution.py:519
  110.7 2.9 %collective-permute-done.5.back1_ref = bf16[272,512]{1,0:T(8,128)(2,1)S(1)} collective-permute-done((bf16[272,512]{1,0:T(8,128)(2,1)S(1)}, bf16[272,512]{1,0:T(8,128)(2,1)S(1)}, u32[]{:S(2)}, u32[]{:S(2)}) %collective-permute-start.5) | collective-permute-done | bytes 278560 | tf_op jit(solution)/shard_map/ppermute | solution.py:371
  (42 shorter events, 10.5 us)
Async XLA Ops:
  0.6 7.0 %copy-start.11 = (bf16[256,512]{1,0:T(8,128)(2,1)S(1)}, bf16[256,512]{1,0:T(8,128)(2,1)}, u32[]{:S(2)}) copy-start(bf16[256,512]{1,0:T(8,128)(2,1)} %refs_0_.4) | copy-start | bytes 786436
  0.6 7.0 %copy-start.12 = (bf16[512,256]{1,0:T(8,128)(2,1)S(1)}, bf16[512,256]{1,0:T(8,128)(2,1)}, u32[]{:S(2)}) copy-start(bf16[512,256]{1,0:T(8,128)(2,1)} %refs_1_.3) | copy-start | bytes 786436
  3.2 4.4 %copy-start.1 = (bf16[4,16,1152]{2,1,0:T(8,128)(2,1)S(1)}, bf16[4,16,1152]{2,1,0:T(8,128)(2,1)}, u32[]{:S(2)}) copy-start(bf16[4,16,1152]{2,1,0:T(8,128)(2,1)} %state.1.refs_2_) | copy-start | bytes 442372
  3.2 10.5 %all-to-all-start = ((bf16[4,16,1152]{2,1,0:T(8,128)(2,1)}), bf16[4,16,1152]{2,1,0:T(8,128)(2,1)S(1)}, u32[]{:S(2)}, u32[]{:S(2)}) async-start(bf16[4,16,1152]{2,1,0:T(8,128)(2,1)} %state.1.refs_2_), calls=%async_computation | async-start | bytes 294912 | tf_op jit(solution)/shard_map/all_to_all | solution.py:375
  7.9 15.5 %copy-start.3 = (bf16[256,1024]{1,0:T(8,128)(2,1)S(1)}, bf16[256,1024]{1,0:T(8,128)(2,1)}, u32[]{:S(2)}) copy-start(bf16[256,1024]{1,0:T(8,128)(2,1)} %refs_2_.1) | copy-start | bytes 1572868
  15.2 8.2 %copy-start.4 = (f32[16,256]{1,0:T(8,128)S(1)}, f32[16,256]{1,0:T(8,128)}, u32[]{:S(2)}) copy-start(f32[16,256]{1,0:T(8,128)} %refs_3_.1) | copy-start | bytes 49156
  15.2 8.2 %copy-start.5 = (bf16[16,256]{1,0:T(8,128)(2,1)S(1)}, bf16[16,256]{1,0:T(8,128)(2,1)}, u32[]{:S(2)}) copy-start(bf16[16,256]{1,0:T(8,128)(2,1)} %refs_4_.1) | copy-start | bytes 24580
  15.2 8.2 %copy-start.6 = (bf16[16,256]{1,0:T(8,128)(2,1)S(1)}, bf16[16,256]{1,0:T(8,128)(2,1)}, u32[]{:S(2)}) copy-start(bf16[16,256]{1,0:T(8,128)(2,1)} %c_ref.1) | copy-start | bytes 24580
  15.2 16.6 %all-to-all-start.1 = ((bf16[8,16,1152]{2,1,0:T(8,128)(2,1)}), bf16[8,16,1152]{2,1,0:T(8,128)(2,1)S(1)}, u32[]{:S(2)}, u32[]{:S(2)}) async-start(bf16[8,16,1152]{2,1,0:T(8,128)(2,1)} %get-tuple-element.12), calls=%async_computation.1 | async-start | bytes 589824 | tf_op jit(solution)/shard_map/all_to_all | solution.py:375
  23.4 0.7 copy-start.13
  24.0 7.8 %copy-start.2 = (bf16[1024,256]{1,0:T(8,128)(2,1)S(1)}, bf16[1024,256]{1,0:T(8,128)(2,1)}, u32[]{:S(2)}) copy-start(bf16[1024,256]{1,0:T(8,128)(2,1)} %w_ref.1) | copy-start | bytes 1572868
  26.3 5.5 %copy-start.7 = (f32[1024]{0:T(1024)S(1)}, f32[1024]{0:T(1024)}, u32[]{:S(2)}) copy-start(f32[1024]{0:T(1024)} %param.20) | copy-start | bytes 12292
  34.4 9.9 %copy-start = (bf16[256,512]{1,0:T(8,128)(2,1)S(1)}, bf16[256,512]{1,0:T(8,128)(2,1)}, u32[]{:S(2)}) copy-start(bf16[256,512]{1,0:T(8,128)(2,1)} %refs_1_.5) | copy-start | bytes 786436
  34.4 18.7 %all-to-all-start.2 = ((bf16[16,16,256]{2,1,0:T(8,128)(2,1)}), bf16[16,16,256]{2,1,0:T(8,128)(2,1)S(1)}, u32[]{:S(2)}, u32[]{:S(2)}) async-start(bf16[16,16,256]{2,1,0:T(8,128)(2,1)} %bitcast.5), calls=%async_computation.2 | async-start | bytes 262144 | tf_op jit(solution)/shard_map/all_to_all | solution.py:375
  54.0 27.7 %all-to-all-start.3 = ((bf16[64,16,256]{2,1,0:T(8,128)(2,1)}), bf16[64,16,256]{2,1,0:T(8,128)(2,1)S(1)}, u32[]{:S(2)}, u32[]{:S(2)}) async-start(bf16[64,16,256]{2,1,0:T(8,128)(2,1)} %sum.1.refs_1_.order_ref), calls=%async_computation.3 | async-start | bytes 1048576 | tf_op jit(solution)/shard_map/all_to_all | solution.py:375
  60.9 10.6 %copy-start.9 = (bf16[256,1024]{1,0:T(8,128)(2,1)S(1)}, bf16[256,1024]{1,0:T(8,128)(2,1)}, u32[]{:S(2)}) copy-start(bf16[256,1024]{1,0:T(8,128)(2,1)} %wk_ref.1) | copy-start | bytes 1572868
  60.9 10.6 %copy-start.10 = (bf16[256,1024]{1,0:T(8,128)(2,1)S(1)}, bf16[256,1024]{1,0:T(8,128)(2,1)}, u32[]{:S(2)}) copy-start(bf16[256,1024]{1,0:T(8,128)(2,1)} %wv_ref.1) | copy-start | bytes 1572868
  60.9 12.0 %collective-permute-start.2 = (bf16[256,512]{1,0:T(8,128)(2,1)S(1)}, bf16[256,512]{1,0:T(8,128)(2,1)S(1)}, u32[]{:S(2)}, u32[]{:S(2)}) collective-permute-start(bf16[256,512]{1,0:T(8,128)(2,1)S(1)} %copy.18), channel_id=1, source_target_pairs={{0,48},{16,32},{32,16},{48,0},{1,49},{17,33},{33,17},{49,1},{2,50}... | collective-permute-start | bytes 786440 | tf_op jit(solution)/shard_map/ppermute | solution.py:371
  64.1 11.0 %collective-permute-start.1 = (bf16[256,512]{1,0:T(8,128)(2,1)S(1)}, bf16[256,512]{1,0:T(8,128)(2,1)S(1)}, u32[]{:S(2)}, u32[]{:S(2)}) collective-permute-start(bf16[256,512]{1,0:T(8,128)(2,1)S(1)} %copy.18), channel_id=1, source_target_pairs={{0,16},{16,0},{32,48},{48,32},{1,17},{17,1},{33,49},{49,33},{2,18}... | collective-permute-start | bytes 786440 | tf_op jit(solution)/shard_map/ppermute | solution.py:371
  66.1 15.6 %collective-permute-start = (bf16[256,512]{1,0:T(8,128)(2,1)S(1)}, bf16[256,512]{1,0:T(8,128)(2,1)S(1)}, u32[]{:S(2)}, u32[]{:S(2)}) collective-permute-start(bf16[256,512]{1,0:T(8,128)(2,1)S(1)} %copy.18), channel_id=1, source_target_pairs={{0,32},{16,48},{32,0},{48,16},{1,33},{17,49},{33,1},{49,17},{2,34}... | collective-permute-start | bytes 786440 | tf_op jit(solution)/shard_map/ppermute | solution.py:371
  82.5 3.8 %collective-permute-start.3 = (bf16[1024,256]{1,0:T(8,128)(2,1)S(1)}, bf16[1024,256]{1,0:T(8,128)(2,1)S(1)}, u32[]{:S(2)}, u32[]{:S(2)}) collective-permute-start(bf16[1024,256]{1,0:T(8,128)(2,1)S(1)} %rebuild.1.mine_ref), channel_id=1, source_target_pairs={{0,1},{1,0},{2,3},{3,2},{4,5},{5,4},{6,7},{7,6},{8,9},{9,8},{10,11... | collective-permute-start | bytes 1572872 | tf_op jit(solution)/shard_map/ppermute | solution.py:371
  89.9 16.0 %collective-permute-start.4 = (bf16[272,512]{1,0:T(8,128)(2,1)S(1)}, bf16[272,512]{1,0:T(8,128)(2,1)S(1)}, u32[]{:S(2)}, u32[]{:S(2)}) collective-permute-start(bf16[272,512]{1,0:T(8,128)(2,1)S(1)} %get-tuple-element.21.refs_4_), channel_id=1, source_target_pairs={{0,32},{16,48},{32,0},{48,16},{1,33},{17,49},{33,1},{49,17},{2,34}... | collective-permute-start | bytes 835592 | tf_op jit(solution)/shard_map/ppermute | solution.py:371
  99.2 11.5 %collective-permute-start.6 = (bf16[272,512]{1,0:T(8,128)(2,1)S(1)}, bf16[272,512]{1,0:T(8,128)(2,1)S(1)}, u32[]{:S(2)}, u32[]{:S(2)}) collective-permute-start(bf16[272,512]{1,0:T(8,128)(2,1)S(1)} %attend.6.refs_4_), channel_id=1, source_target_pairs={{0,48},{16,32},{32,16},{48,0},{1,49},{17,33},{33,17},{49,1},{2,50}... | collective-permute-start | bytes 835592 | tf_op jit(solution)/shard_map/ppermute | solution.py:371
  103.6 10.0 %collective-permute-start.5 = (bf16[272,512]{1,0:T(8,128)(2,1)S(1)}, bf16[272,512]{1,0:T(8,128)(2,1)S(1)}, u32[]{:S(2)}, u32[]{:S(2)}) collective-permute-start(bf16[272,512]{1,0:T(8,128)(2,1)S(1)} %attend.5.refs_4_), channel_id=1, source_target_pairs={{0,16},{16,0},{32,48},{48,32},{1,17},{17,1},{33,49},{49,33},{2,18}... | collective-permute-start | bytes 835592 | tf_op jit(solution)/shard_map/ppermute | solution.py:371
  (1 other events, 0.7 us)

commit v2 on v1

--- a/solution.py
+++ b/solution.py
@@ -261,9 +261,7 @@
         key = (slot // PIECE) * (2 * PIECE) + own * PIECE + (slot & (PIECE - 1))
         allowed.append(key <= token)
 
-    allowed = [jnp.concatenate([part, part], axis=0) for part in allowed]
-
-    def scored(first, part):
+    def scored(first):
         query = jnp.concatenate(
             [
                 jnp.concatenate([q_ref[:, h * HD : (h + 1) * HD], unit], axis=1)
@@ -271,35 +269,26 @@
             ],
             axis=0,
         )
-        scores = lax.dot_general(
-            query,
-            k_ref[part * NY * HALF : (part + 1) * NY * HALF, :],
-            (((1,), (1,)), ((), ())),
-            preferred_element_type=F32,
+        return lax.dot_general(
+            query, k_ref[...], (((1,), (1,)), ((), ())), preferred_element_type=F32
         )
-        near = jnp.where(allowed[part], scores[:, :HALF], NEG_BIG)
-        return jnp.concatenate([near, scores[:, HALF:]], axis=1)
-
+
+    allowed = [jnp.concatenate([part, part], axis=0) for part in allowed]
     stats = jnp.zeros((ROWS, 128), F32)
-    following = scored(0, 0)
+    following = scored(0)
     for first in range(0, HEADS_Q, 2):
-        best = sums = None
+        scores = following
+        if first + 2 < HEADS_Q:
+            following = scored(first + 2)
+        pieces = []
         for part in range(2):
-            scores = following
-            if part == 0:
-                following = scored(first, 1)
-            elif first + 2 < HEADS_Q:
-                following = scored(first + 2, 0)
-            chunk_best = jnp.max(scores, axis=1, keepdims=True)
-            values = v_ref[part * NY * HALF : (part + 1) * NY * HALF, :]
-            if part == 0:
-                best = chunk_best
-                sums = dot(jnp.exp2(scores - best).astype(BF16), values)
-            else:
-                old, best = best, jnp.maximum(best, chunk_best)
-                sums = sums * jnp.exp2(old - best) + dot(
-                    jnp.exp2(scores - best).astype(BF16), values
-                )
+            begin = part * NY * HALF
+            pieces.append(jnp.where(allowed[part], scores[:, begin : begin + HALF], NEG_BIG))
+            pieces.append(scores[:, begin + HALF : begin + NY * HALF])
+        scores = jnp.concatenate(pieces, axis=1)
+        best = jnp.max(scores, axis=1, keepdims=True)
+        weights = jnp.exp2(scores - best).astype(BF16)
+        sums = dot(weights, v_ref[...])
         norm = sums[:, HD:]
         ratio = (sums[:, :HD] / norm).astype(BF16)
         level = best + jnp.log2(norm)
@@ -477,7 +466,9 @@
 
     blocks = exchange(latents, ("y", "z")).reshape(NY, HALF, RANK)
     lent = copied(latents)
-    visiting1, visiting2, visiting3 = [swap(lent, "x", NX, k) for k in (1, 2, 3)]
+    visiting1 = swap(lent, "x", NX, 1)
+    visiting3 = swap(lent, "x", NX, 3)
+    visiting2 = swap(visiting1, "x", NX, 3)
     weights = pl.pallas_call(
         weights_kernel,
         out_shape=shape((RANK, 2 * HD), BF16),

time: 116 us -> 116 us (level)
  the two profiles are of different devices: /device:TPU:16 before, /device:TPU:2 now
where the time goes in v2:
time: 116 us; the launch traced here: 115 us
  starting transfers between devices  48.4 us (42%)
  waiting for transfers between devices  39.4 us (34%)
  Pallas kernels  25.6 us (22%)
    all_to_all x4, starting transfers between devices, exchange(): return lax.all_to_all(chunks, axes, 0, 0, tiled=True)  27.8 us
    all_to_all x4, waiting for transfers between devices, exchange(): return lax.all_to_all(chunks, axes, 0, 0, tiled=True)  20.8 us
    ppermute x7, starting transfers between devices, swap(): return lax.ppermute(value, axis, [(i, i ^ step) for i in range(size)])  20.7 us
    ppermute x7, waiting for transfers between devices, swap(): return lax.ppermute(value, axis, [(i, i ^ step) for i in range(size)])  18.6 us
    pallas_call x3, Pallas kernels, body(): call(after(kernel, 4), 'attend', answer, [SM, VM, VM, VM] + [ANY] * (len(...  9.35 us
    pallas_call x1, Pallas kernels, body(): call(functools.partial(attend_first_kernel, 2), 'attend', (answer, wide,...  3.34 us
    pallas_call x1, Pallas kernels, body(): call(finish_kernel, 'finish', (shape((ROWS, INNER), BF16), shape((ROWS, R...  2.62 us
    pallas_call x1, Pallas kernels, body(): call(state_kernel, 'state', shape((NX, STATE, PAY), BF16), [SM, (ROWS, IN...  2.59 us
  transfers between devices with their start and end apart: 11, of which 9 were waited for; matrix products, arithmetic and copies ran while one was open for 0% of the time, Pallas kernels for 11%

profile of v2, /device:TPU:2, one launch (start us, length us, event | category | flops | bytes accessed | tf_op | source)
XLA Modules:
  0.0 115.1 jit_solution(16989238073638946162)
XLA Ops:
  0.6 2.6 %state.1.refs_2_ = bf16[4,16,1152]{2,1,0:T(8,128)(2,1)} custom-call(f32[16]{0:T(128)} %refs_0_.5, bf16[256,1024]{1,0:T(8,128)(2,1)} %refs_2_.1, f32[16,256]{1,0:T(8,128)} %refs_3_.1, bf16[16,256]{1,0:T(8,128)(2,1)} %refs_4_.1), custom_call_target="tpu_custom_call" | custom-call | flops 134217728 | bytes 1048576 | tf_op jit(solution)/shard_map/state/pallas_call | solution.py:393
  3.2 9.3 %all-to-all-start = ((bf16[4,16,1152]{2,1,0:T(8,128)(2,1)}), bf16[4,16,1152]{2,1,0:T(8,128)(2,1)S(1)}, u32[]{:S(2)}, u32[]{:S(2)}) async-start(bf16[4,16,1152]{2,1,0:T(8,128)(2,1)} %state.1.refs_2_), calls=%async_computation | async-start | bytes 294912 | tf_op jit(solution)/shard_map/all_to_all | solution.py:364
  12.9 4.3 %all-to-all-done.refs_1_ = bf16[4,16,1152]{2,1,0:T(8,128)(2,1)S(1)} async-done(((bf16[4,16,1152]{2,1,0:T(8,128)(2,1)}), bf16[4,16,1152]{2,1,0:T(8,128)(2,1)S(1)}, u32[]{:S(2)}, u32[]{:S(2)}) %all-to-all-start) | async-done | bytes 147488 | tf_op jit(solution)/shard_map/all_to_all | solution.py:364
  18.6 3.6 %all-to-all-start.1 = ((bf16[8,16,1152]{2,1,0:T(8,128)(2,1)}), bf16[8,16,1152]{2,1,0:T(8,128)(2,1)S(1)}, u32[]{:S(2)}, u32[]{:S(2)}) async-start(bf16[8,16,1152]{2,1,0:T(8,128)(2,1)} %get-tuple-element.12), calls=%async_computation.1 | async-start | bytes 589824 | tf_op jit(solution)/shard_map/all_to_all | solution.py:364
  22.9 2.2 %intra.1 = (f32[256,1024]{1,0:T(8,128)S(1)}, bf16[256,128]{1,0:T(8,128)(2,1)S(1)}) custom-call(f32[16]{0:T(128)S(1)} %copy-done.8, f32[16]{0:T(128)S(1)} %copy-done.13, bf16[256,1024]{1,0:T(8,128)(2,1)S(1)} %copy-done.3, f32[16,256]{1,0:T(8,128)S(1)} %copy-done.4, bf16[16,256]{1,0:T(8,128)(2,1)S(1)} %copy-done.5, bf16[16,256]{1,0:T(8,128)(2,1)S(1)} %copy-done.6, ...), custom_call_target="tpu_custom_call" | custom-call | flops 2147483648 | bytes 3145728 | tf_op jit(solution)/shard_map/intra/pallas_call | solution.py:428
  25.2 7.8 %all-to-all-done.1.rows_ref = bf16[8,16,1152]{2,1,0:T(8,128)(2,1)S(1)} async-done(((bf16[8,16,1152]{2,1,0:T(8,128)(2,1)}), bf16[8,16,1152]{2,1,0:T(8,128)(2,1)S(1)}, u32[]{:S(2)}, u32[]{:S(2)}) %all-to-all-start.1) | async-done | bytes 294944 | tf_op jit(solution)/shard_map/all_to_all | solution.py:364
  33.0 2.6 %finish.1 = (bf16[256,1024]{1,0:T(8,128)(2,1)}, bf16[256,256]{1,0:T(8,128)(2,1)}) custom-call(s32[4]{0:T(128)S(1)} %pad_add_fusion.refs_0_.place_ref, bf16[8,16,1152]{2,1,0:T(8,128)(2,1)S(1)} %all-to-all-done.1.rows_ref, f32[16,1024]{1,0:T(8,128)S(1)} %get-tuple-element.13.refs_6_.before_ref, f32[16,1024]{1,0:T(8,128)S(1)} %get-tuple-element.14.decay_ref, ...), custom_call_target="tpu_custom_call" | custom-call | flops 536870912 | bytes 4194304 | tf_op jit(solution)/shard_map/finish/pallas_call | solution.py:437
  35.6 10.2 %all-to-all-start.2 = ((bf16[16,16,256]{2,1,0:T(8,128)(2,1)}), bf16[16,16,256]{2,1,0:T(8,128)(2,1)S(1)}, u32[]{:S(2)}, u32[]{:S(2)}) async-start(bf16[16,16,256]{2,1,0:T(8,128)(2,1)} %bitcast.5), calls=%async_computation.2 | async-start | bytes 262144 | tf_op jit(solution)/shard_map/all_to_all | solution.py:364
  45.9 8.7 %all-to-all-done.2.refs_0_ = bf16[16,16,256]{2,1,0:T(8,128)(2,1)S(1)} async-done(((bf16[16,16,256]{2,1,0:T(8,128)(2,1)}), bf16[16,16,256]{2,1,0:T(8,128)(2,1)S(1)}, u32[]{:S(2)}, u32[]{:S(2)}) %all-to-all-start.2) | async-done | bytes 131104 | tf_op jit(solution)/shard_map/all_to_all | solution.py:364
  55.4 4.6 %all-to-all-start.3 = ((bf16[64,16,256]{2,1,0:T(8,128)(2,1)}), bf16[64,16,256]{2,1,0:T(8,128)(2,1)S(1)}, u32[]{:S(2)}, u32[]{:S(2)}) async-start(bf16[64,16,256]{2,1,0:T(8,128)(2,1)} %sum.1.refs_1_.order_ref), calls=%async_computation.3 | async-start | bytes 1048576 | tf_op jit(solution)/shard_map/all_to_all | solution.py:364
  60.1 3.5 %collective-permute-start = (bf16[256,512]{1,0:T(8,128)(2,1)S(1)}, bf16[256,512]{1,0:T(8,128)(2,1)S(1)}, u32[]{:S(2)}, u32[]{:S(2)}) collective-permute-start(bf16[256,512]{1,0:T(8,128)(2,1)S(1)} %copy.18), channel_id=1, source_target_pairs={{0,16},{16,0},{32,48},{48,32},{1,17},{17,1},{33,49},{49,33},{2,18}... | collective-permute-start | bytes 786440 | tf_op jit(solution)/shard_map/ppermute | solution.py:360
  63.6 2.5 %collective-permute-start.2 = (bf16[256,512]{1,0:T(8,128)(2,1)S(1)}, bf16[256,512]{1,0:T(8,128)(2,1)S(1)}, u32[]{:S(2)}, u32[]{:S(2)}) collective-permute-start(bf16[256,512]{1,0:T(8,128)(2,1)S(1)} %copy.18), channel_id=1, source_target_pairs={{0,48},{16,32},{32,16},{48,0},{1,49},{17,33},{33,17},{49,1},{2,50}... | collective-permute-start | bytes 786440 | tf_op jit(solution)/shard_map/ppermute | solution.py:360
  66.1 5.1 %collective-permute-done.refs_3_.refs_1_ = bf16[256,512]{1,0:T(8,128)(2,1)S(1)} collective-permute-done((bf16[256,512]{1,0:T(8,128)(2,1)S(1)}, bf16[256,512]{1,0:T(8,128)(2,1)S(1)}, u32[]{:S(2)}, u32[]{:S(2)}) %collective-permute-start) | collective-permute-done | bytes 262176 | tf_op jit(solution)/shard_map/ppermute | solution.py:360
  71.2 2.2 %collective-permute-start.1 = (bf16[256,512]{1,0:T(8,128)(2,1)S(1)}, bf16[256,512]{1,0:T(8,128)(2,1)S(1)}, u32[]{:S(2)}, u32[]{:S(2)}) collective-permute-start(bf16[256,512]{1,0:T(8,128)(2,1)S(1)} %collective-permute-done.refs_3_.refs_1_), channel_id=1, source_target_pairs={{0,48},{16,32},{32,16},{48,0},{1,49},{17,33},{33,17},{49,1},{2,50}... | collective-permute-start | bytes 786440 | tf_op jit(solution)/shard_map/ppermute | solution.py:360
  74.3 7.0 %collective-permute-done.1.refs_4_.q_ref = bf16[256,512]{1,0:T(8,128)(2,1)S(1)} collective-permute-done((bf16[256,512]{1,0:T(8,128)(2,1)S(1)}, bf16[256,512]{1,0:T(8,128)(2,1)S(1)}, u32[]{:S(2)}, u32[]{:S(2)}) %collective-permute-start.1) | collective-permute-done | bytes 262176 | tf_op jit(solution)/shard_map/ppermute | solution.py:360
  82.1 1.9 %collective-permute-start.3 = (bf16[1024,256]{1,0:T(8,128)(2,1)S(1)}, bf16[1024,256]{1,0:T(8,128)(2,1)S(1)}, u32[]{:S(2)}, u32[]{:S(2)}) collective-permute-start(bf16[1024,256]{1,0:T(8,128)(2,1)S(1)} %rebuild.1.mine_ref), channel_id=1, source_target_pairs={{0,1},{1,0},{2,3},{3,2},{4,5},{5,4},{6,7},{7,6},{8,9},{9,8},{10,11... | collective-permute-start | bytes 1572872 | tf_op jit(solution)/shard_map/ppermute | solution.py:360
  85.9 3.3 %attend.4 = (bf16[272,512]{1,0:T(8,128)(2,1)S(1)}, bf16[2048,256]{1,0:T(8,128)(2,1)S(1)}, bf16[2048,256]{1,0:T(8,128)(2,1)S(1)}) custom-call(s32[4]{0:T(128)S(1)} %pad_add_fusion.refs_0_.place_ref, bf16[256,512]{1,0:T(8,128)(2,1)S(1)} %collective-permute-done.1.refs_4_.q_ref, bf16[1024,256]{1,0:T(8,128)(2,1)S(1)} %rebuild.1.mine_ref, ...), custom_call_target="tpu_custom_call" | custom-call | flops 1073741824 | bytes 4194304 | tf_op jit(solution)/shard_map/attend/pallas_call | solution.py:499
  89.3 4.8 %collective-permute-start.4 = (bf16[272,512]{1,0:T(8,128)(2,1)S(1)}, bf16[272,512]{1,0:T(8,128)(2,1)S(1)}, u32[]{:S(2)}, u32[]{:S(2)}) collective-permute-start(bf16[272,512]{1,0:T(8,128)(2,1)S(1)} %get-tuple-element.21.refs_4_), channel_id=1, source_target_pairs={{0,32},{16,48},{32,0},{48,16},{1,33},{17,49},{33,1},{49,17},{2,34}... | collective-permute-start | bytes 835592 | tf_op jit(solution)/shard_map/ppermute | solution.py:360
  94.0 3.1 %attend.5.refs_4_ = bf16[272,512]{1,0:T(8,128)(2,1)S(1)} custom-call(s32[4]{0:T(128)S(1)} %pad_add_fusion.refs_0_.place_ref, bf16[256,512]{1,0:T(8,128)(2,1)S(1)} %collective-permute-done.refs_3_.refs_1_, bf16[2048,256]{1,0:T(8,128)(2,1)S(1)} %get-tuple-element.19.refs_2_, bf16[2048,256]{1,0:T(8,128)(2,1)S(1)} %get-tuple-element.20.refs_3_, ...), custom_call_target="tpu_custom_call" | custom-call | flops 1073741824 | bytes 4194304 | tf_op jit(solution)/shard_map/attend/pallas_call | solution.py:510
  97.1 3.1 %attend.6.refs_4_ = bf16[272,512]{1,0:T(8,128)(2,1)S(1)} custom-call(s32[4]{0:T(128)S(1)} %pad_add_fusion.refs_0_.place_ref, bf16[256,512]{1,0:T(8,128)(2,1)S(1)} %collective-permute-done.2.refs_5_.refs_1_, bf16[2048,256]{1,0:T(8,128)(2,1)S(1)} %get-tuple-element.19.refs_2_, bf16[2048,256]{1,0:T(8,128)(2,1)S(1)} %get-tuple-element.20.refs_3_, ...), custom_call_target="tpu_custom_call" | custom-call | flops 1073741824 | bytes 4194304 | tf_op jit(solution)/shard_map/attend/pallas_call | solution.py:510
  100.3 3.4 %collective-permute-start.6 = (bf16[272,512]{1,0:T(8,128)(2,1)S(1)}, bf16[272,512]{1,0:T(8,128)(2,1)S(1)}, u32[]{:S(2)}, u32[]{:S(2)}) collective-permute-start(bf16[272,512]{1,0:T(8,128)(2,1)S(1)} %attend.6.refs_4_), channel_id=1, source_target_pairs={{0,48},{16,32},{32,16},{48,0},{1,49},{17,33},{33,17},{49,1},{2,50}... | collective-permute-start | bytes 835592 | tf_op jit(solution)/shard_map/ppermute | solution.py:360
  103.6 2.5 %collective-permute-start.5 = (bf16[272,512]{1,0:T(8,128)(2,1)S(1)}, bf16[272,512]{1,0:T(8,128)(2,1)S(1)}, u32[]{:S(2)}, u32[]{:S(2)}) collective-permute-start(bf16[272,512]{1,0:T(8,128)(2,1)S(1)} %attend.5.refs_4_), channel_id=1, source_target_pairs={{0,16},{16,0},{32,48},{48,32},{1,17},{17,1},{33,49},{49,33},{2,18}... | collective-permute-start | bytes 835592 | tf_op jit(solution)/shard_map/ppermute | solution.py:360
  106.1 3.1 %attend.7.own_ref = bf16[272,512]{1,0:T(8,128)(2,1)S(1)} custom-call(s32[4]{0:T(128)S(1)} %pad_add_fusion.refs_0_.place_ref, bf16[256,512]{1,0:T(8,128)(2,1)S(1)} %copy-done, bf16[2048,256]{1,0:T(8,128)(2,1)S(1)} %get-tuple-element.19.refs_2_, bf16[2048,256]{1,0:T(8,128)(2,1)S(1)} %get-tuple-element.20.refs_3_, bf16[272,512]{1,0:T(8,128)(2,1)S(1)} %attend.6.refs_4_, ...), custom_call_target="tpu_custom_call" | custom-call | flops 1073741824 | bytes 4194304 | tf_op jit(solution)/shard_map/attend/pallas_call | solution.py:510
  110.6 3.1 %collective-permute-done.5.back1_ref = bf16[272,512]{1,0:T(8,128)(2,1)S(1)} collective-permute-done((bf16[272,512]{1,0:T(8,128)(2,1)S(1)}, bf16[272,512]{1,0:T(8,128)(2,1)S(1)}, u32[]{:S(2)}, u32[]{:S(2)}) %collective-permute-start.5) | collective-permute-done | bytes 278560 | tf_op jit(solution)/shard_map/ppermute | solution.py:360
  (42 shorter events, 9.7 us)
Async XLA Ops:
  0.6 12.0 %copy-start.11 = (bf16[256,512]{1,0:T(8,128)(2,1)S(1)}, bf16[256,512]{1,0:T(8,128)(2,1)}, u32[]{:S(2)}) copy-start(bf16[256,512]{1,0:T(8,128)(2,1)} %refs_0_.4) | copy-start | bytes 786436
  0.6 11.9 %copy-start.12 = (bf16[512,256]{1,0:T(8,128)(2,1)S(1)}, bf16[512,256]{1,0:T(8,128)(2,1)}, u32[]{:S(2)}) copy-start(bf16[512,256]{1,0:T(8,128)(2,1)} %refs_1_.3) | copy-start | bytes 786436
  3.2 9.4 %copy-start.1 = (bf16[4,16,1152]{2,1,0:T(8,128)(2,1)S(1)}, bf16[4,16,1152]{2,1,0:T(8,128)(2,1)}, u32[]{:S(2)}) copy-start(bf16[4,16,1152]{2,1,0:T(8,128)(2,1)} %state.1.refs_2_) | copy-start | bytes 442372
  3.2 14.0 %all-to-all-start = ((bf16[4,16,1152]{2,1,0:T(8,128)(2,1)}), bf16[4,16,1152]{2,1,0:T(8,128)(2,1)S(1)}, u32[]{:S(2)}, u32[]{:S(2)}) async-start(bf16[4,16,1152]{2,1,0:T(8,128)(2,1)} %state.1.refs_2_), calls=%async_computation | async-start | bytes 294912 | tf_op jit(solution)/shard_map/all_to_all | solution.py:364
  12.8 9.4 %copy-start.3 = (bf16[256,1024]{1,0:T(8,128)(2,1)S(1)}, bf16[256,1024]{1,0:T(8,128)(2,1)}, u32[]{:S(2)}) copy-start(bf16[256,1024]{1,0:T(8,128)(2,1)} %refs_2_.1) | copy-start | bytes 1572868
  18.6 3.6 %copy-start.4 = (f32[16,256]{1,0:T(8,128)S(1)}, f32[16,256]{1,0:T(8,128)}, u32[]{:S(2)}) copy-start(f32[16,256]{1,0:T(8,128)} %refs_3_.1) | copy-start | bytes 49156
  18.6 3.6 %copy-start.5 = (bf16[16,256]{1,0:T(8,128)(2,1)S(1)}, bf16[16,256]{1,0:T(8,128)(2,1)}, u32[]{:S(2)}) copy-start(bf16[16,256]{1,0:T(8,128)(2,1)} %refs_4_.1) | copy-start | bytes 24580
  18.6 3.6 %copy-start.6 = (bf16[16,256]{1,0:T(8,128)(2,1)S(1)}, bf16[16,256]{1,0:T(8,128)(2,1)}, u32[]{:S(2)}) copy-start(bf16[16,256]{1,0:T(8,128)(2,1)} %c_ref.1) | copy-start | bytes 24580
  18.6 14.3 %all-to-all-start.1 = ((bf16[8,16,1152]{2,1,0:T(8,128)(2,1)}), bf16[8,16,1152]{2,1,0:T(8,128)(2,1)S(1)}, u32[]{:S(2)}, u32[]{:S(2)}) async-start(bf16[8,16,1152]{2,1,0:T(8,128)(2,1)} %get-tuple-element.12), calls=%async_computation.1 | async-start | bytes 589824 | tf_op jit(solution)/shard_map/all_to_all | solution.py:364
  22.2 0.7 copy-start.13
  22.9 10.1 %copy-start.2 = (bf16[1024,256]{1,0:T(8,128)(2,1)S(1)}, bf16[1024,256]{1,0:T(8,128)(2,1)}, u32[]{:S(2)}) copy-start(bf16[1024,256]{1,0:T(8,128)(2,1)} %w_ref.1) | copy-start | bytes 1572868
  25.1 7.8 %copy-start.7 = (f32[1024]{0:T(1024)S(1)}, f32[1024]{0:T(1024)}, u32[]{:S(2)}) copy-start(f32[1024]{0:T(1024)} %param.20) | copy-start | bytes 12292
  35.6 10.2 %copy-start = (bf16[256,512]{1,0:T(8,128)(2,1)S(1)}, bf16[256,512]{1,0:T(8,128)(2,1)}, u32[]{:S(2)}) copy-start(bf16[256,512]{1,0:T(8,128)(2,1)} %refs_1_.5) | copy-start | bytes 786436
  35.6 19.0 %all-to-all-start.2 = ((bf16[16,16,256]{2,1,0:T(8,128)(2,1)}), bf16[16,16,256]{2,1,0:T(8,128)(2,1)S(1)}, u32[]{:S(2)}, u32[]{:S(2)}) async-start(bf16[16,16,256]{2,1,0:T(8,128)(2,1)} %bitcast.5), calls=%async_computation.2 | async-start | bytes 262144 | tf_op jit(solution)/shard_map/all_to_all | solution.py:364
  55.4 25.8 %all-to-all-start.3 = ((bf16[64,16,256]{2,1,0:T(8,128)(2,1)}), bf16[64,16,256]{2,1,0:T(8,128)(2,1)S(1)}, u32[]{:S(2)}, u32[]{:S(2)}) async-start(bf16[64,16,256]{2,1,0:T(8,128)(2,1)} %sum.1.refs_1_.order_ref), calls=%async_computation.3 | async-start | bytes 1048576 | tf_op jit(solution)/shard_map/all_to_all | solution.py:364
  60.1 13.3 %copy-start.9 = (bf16[256,1024]{1,0:T(8,128)(2,1)S(1)}, bf16[256,1024]{1,0:T(8,128)(2,1)}, u32[]{:S(2)}) copy-start(bf16[256,1024]{1,0:T(8,128)(2,1)} %wk_ref.1) | copy-start | bytes 1572868
  60.1 13.3 %copy-start.10 = (bf16[256,1024]{1,0:T(8,128)(2,1)S(1)}, bf16[256,1024]{1,0:T(8,128)(2,1)}, u32[]{:S(2)}) copy-start(bf16[256,1024]{1,0:T(8,128)(2,1)} %wv_ref.1) | copy-start | bytes 1572868
  60.1 11.1 %collective-permute-start = (bf16[256,512]{1,0:T(8,128)(2,1)S(1)}, bf16[256,512]{1,0:T(8,128)(2,1)S(1)}, u32[]{:S(2)}, u32[]{:S(2)}) collective-permute-start(bf16[256,512]{1,0:T(8,128)(2,1)S(1)} %copy.18), channel_id=1, source_target_pairs={{0,16},{16,0},{32,48},{48,32},{1,17},{17,1},{33,49},{49,33},{2,18}... | collective-permute-start | bytes 786440 | tf_op jit(solution)/shard_map/ppermute | solution.py:360
  63.6 10.7 %collective-permute-start.2 = (bf16[256,512]{1,0:T(8,128)(2,1)S(1)}, bf16[256,512]{1,0:T(8,128)(2,1)S(1)}, u32[]{:S(2)}, u32[]{:S(2)}) collective-permute-start(bf16[256,512]{1,0:T(8,128)(2,1)S(1)} %copy.18), channel_id=1, source_target_pairs={{0,48},{16,32},{32,16},{48,0},{1,49},{17,33},{33,17},{49,1},{2,50}... | collective-permute-start | bytes 786440 | tf_op jit(solution)/shard_map/ppermute | solution.py:360
  71.2 10.1 %collective-permute-start.1 = (bf16[256,512]{1,0:T(8,128)(2,1)S(1)}, bf16[256,512]{1,0:T(8,128)(2,1)S(1)}, u32[]{:S(2)}, u32[]{:S(2)}) collective-permute-start(bf16[256,512]{1,0:T(8,128)(2,1)S(1)} %collective-permute-done.refs_3_.refs_1_), channel_id=1, source_target_pairs={{0,48},{16,32},{32,16},{48,0},{1,49},{17,33},{33,17},{49,1},{2,50}... | collective-permute-start | bytes 786440 | tf_op jit(solution)/shard_map/ppermute | solution.py:360
  82.1 3.8 %collective-permute-start.3 = (bf16[1024,256]{1,0:T(8,128)(2,1)S(1)}, bf16[1024,256]{1,0:T(8,128)(2,1)S(1)}, u32[]{:S(2)}, u32[]{:S(2)}) collective-permute-start(bf16[1024,256]{1,0:T(8,128)(2,1)S(1)} %rebuild.1.mine_ref), channel_id=1, source_target_pairs={{0,1},{1,0},{2,3},{3,2},{4,5},{5,4},{6,7},{7,6},{8,9},{9,8},{10,11... | collective-permute-start | bytes 1572872 | tf_op jit(solution)/shard_map/ppermute | solution.py:360
  89.3 16.9 %collective-permute-start.4 = (bf16[272,512]{1,0:T(8,128)(2,1)S(1)}, bf16[272,512]{1,0:T(8,128)(2,1)S(1)}, u32[]{:S(2)}, u32[]{:S(2)}) collective-permute-start(bf16[272,512]{1,0:T(8,128)(2,1)S(1)} %get-tuple-element.21.refs_4_), channel_id=1, source_target_pairs={{0,32},{16,48},{32,0},{48,16},{1,33},{17,49},{33,1},{49,17},{2,34}... | collective-permute-start | bytes 835592 | tf_op jit(solution)/shard_map/ppermute | solution.py:360
  100.3 10.3 %collective-permute-start.6 = (bf16[272,512]{1,0:T(8,128)(2,1)S(1)}, bf16[272,512]{1,0:T(8,128)(2,1)S(1)}, u32[]{:S(2)}, u32[]{:S(2)}) collective-permute-start(bf16[272,512]{1,0:T(8,128)(2,1)S(1)} %attend.6.refs_4_), channel_id=1, source_target_pairs={{0,48},{16,32},{32,16},{48,0},{1,49},{17,33},{33,17},{49,1},{2,50}... | collective-permute-start | bytes 835592 | tf_op jit(solution)/shard_map/ppermute | solution.py:360
  103.6 10.0 %collective-permute-start.5 = (bf16[272,512]{1,0:T(8,128)(2,1)S(1)}, bf16[272,512]{1,0:T(8,128)(2,1)S(1)}, u32[]{:S(2)}, u32[]{:S(2)}) collective-permute-start(bf16[272,512]{1,0:T(8,128)(2,1)S(1)} %attend.5.refs_4_), channel_id=1, source_target_pairs={{0,16},{16,0},{32,48},{48,32},{1,17},{17,1},{33,49},{49,33},{2,18}... | collective-permute-start | bytes 835592 | tf_op jit(solution)/shard_map/ppermute | solution.py:360
  (1 other events, 0.7 us)

commit v3 on v2

--- a/solution.py
+++ b/solution.py
@@ -287,7 +287,7 @@
             pieces.append(scores[:, begin + HALF : begin + NY * HALF])
         scores = jnp.concatenate(pieces, axis=1)
         best = jnp.max(scores, axis=1, keepdims=True)
-        weights = jnp.exp2(scores - best).astype(BF16)
+        weights = jnp.exp2((scores - best).astype(BF16))
         sums = dot(weights, v_ref[...])
         norm = sums[:, HD:]
         ratio = (sums[:, :HD] / norm).astype(BF16)
@@ -483,25 +483,25 @@
         compiler_params=pltpu.CompilerParams(vmem_limit_bytes=8 * MIB),
     )(place, key_rebuild, value_rebuild, latents)
     mine = call(
-        after(after(after(rebuild_kernel, 3), 3), 3),
+        after(after(rebuild_kernel, 3), 3),
         "rebuild",
         shape((NY * HALF, 2 * HD), BF16),
-        [SM, VM, VM, ANY, ANY, ANY],
+        [SM, VM, VM, ANY, ANY],
         8,
         1 << 27,
         MIB,
-    )(place, blocks, weights, visiting1, visiting2, visiting3)
+    )(place, blocks, weights, visiting1, visiting3)
     other = swap(mine, "core", NC, 1)
 
     work = 4 * ROWS * HEADS_Q * HD * NY * ROWS
     answer = shape((ROWS + 16, HEADS_Q * HD), BF16)
     wide = shape((NY * ROWS, 2 * HD), BF16)
     done, keys, values = call(
-        functools.partial(attend_first_kernel, 2), "attend", (answer, wide, wide),
+        functools.partial(attend_first_kernel, 1), "attend", (answer, wide, wide),
         [SM, VM, VM, VM], 24, work, 4 * MIB,
-    )(place, visiting2, mine, other)
-    back = {2: swap(done, "x", NX, 2)}
-    for step, query, awaited in ((1, visiting1, None), (3, visiting3, None), (0, queries, 2)):
+    )(place, visiting1, mine, other)
+    back = {1: swap(done, "x", NX, 1)}
+    for step, query, awaited in ((2, visiting2, None), (3, visiting3, 1), (0, queries, None)):
         kernel = functools.partial(attend_kernel, step)
         operands = [place, query, keys, values, done]
         if awaited is not None:

time: 116 us -> 119 us (1.026)
  the two profiles are of different devices: /device:TPU:2 before, /device:TPU:16 now
where the time goes in v3:
time: 119 us
  starting transfers between devices  47.8 us (40%)
  waiting for transfers between devices  42.4 us (36%)
  Pallas kernels  26.7 us (22%)
    all_to_all x4, starting transfers between devices, exchange(): return lax.all_to_all(chunks, axes, 0, 0, tiled=True)  29.4 us
    all_to_all x4, waiting for transfers between devices, exchange(): return lax.all_to_all(chunks, axes, 0, 0, tiled=True)  26.3 us
    ppermute x7, starting transfers between devices, swap(): return lax.ppermute(value, axis, [(i, i ^ step) for i in range(size)])  18.4 us
    ppermute x7, waiting for transfers between devices, swap(): return lax.ppermute(value, axis, [(i, i ^ step) for i in range(size)])  16.1 us
    pallas_call x3, Pallas kernels, body(): call(after(kernel, 4), 'attend', answer, [SM, VM, VM, VM] + [ANY] * (len(...  10.1 us
    pallas_call x1, Pallas kernels, body(): call(functools.partial(attend_first_kernel, 1), 'attend', (answer, wide,...  3.64 us
    pallas_call x1, Pallas kernels, body(): call(finish_kernel, 'finish', (shape((ROWS, INNER), BF16), shape((ROWS, R...  2.61 us
    pallas_call x1, Pallas kernels, body(): call(state_kernel, 'state', shape((NX, STATE, PAY), BF16), [SM, (ROWS, IN...  2.59 us
  transfers between devices with their start and end apart: 11, of which 8 were waited for; matrix products, arithmetic and copies ran while one was open for 0% of the time, Pallas kernels for 14%

profile of v3, /device:TPU:16, one launch (start us, length us, event | category | flops | bytes accessed | tf_op | source)
XLA Modules:
  0.0 118.6 jit_solution(8219894945468285562)
XLA Ops:
  0.6 2.6 %state.1.refs_2_ = bf16[4,16,1152]{2,1,0:T(8,128)(2,1)} custom-call(f32[16]{0:T(128)} %refs_0_.5, bf16[256,1024]{1,0:T(8,128)(2,1)} %refs_2_.1, f32[16,256]{1,0:T(8,128)} %refs_3_.1, bf16[16,256]{1,0:T(8,128)(2,1)} %refs_4_.1), custom_call_target="tpu_custom_call" | custom-call | flops 134217728 | bytes 1048576 | tf_op jit(solution)/shard_map/state/pallas_call | solution.py:393
  3.2 4.4 %all-to-all-start = ((bf16[4,16,1152]{2,1,0:T(8,128)(2,1)}), bf16[4,16,1152]{2,1,0:T(8,128)(2,1)S(1)}, u32[]{:S(2)}, u32[]{:S(2)}) async-start(bf16[4,16,1152]{2,1,0:T(8,128)(2,1)} %state.1.refs_2_), calls=%async_computation | async-start | bytes 294912 | tf_op jit(solution)/shard_map/all_to_all | solution.py:364
  8.0 5.7 %all-to-all-done.refs_1_ = bf16[4,16,1152]{2,1,0:T(8,128)(2,1)S(1)} async-done(((bf16[4,16,1152]{2,1,0:T(8,128)(2,1)}), bf16[4,16,1152]{2,1,0:T(8,128)(2,1)S(1)}, u32[]{:S(2)}, u32[]{:S(2)}) %all-to-all-start) | async-done | bytes 147488 | tf_op jit(solution)/shard_map/all_to_all | solution.py:364
  15.2 8.2 %all-to-all-start.1 = ((bf16[8,16,1152]{2,1,0:T(8,128)(2,1)}), bf16[8,16,1152]{2,1,0:T(8,128)(2,1)S(1)}, u32[]{:S(2)}, u32[]{:S(2)}) async-start(bf16[8,16,1152]{2,1,0:T(8,128)(2,1)} %get-tuple-element.12), calls=%async_computation.1 | async-start | bytes 589824 | tf_op jit(solution)/shard_map/all_to_all | solution.py:364
  24.0 2.2 %intra.1 = (f32[256,1024]{1,0:T(8,128)S(1)}, bf16[256,128]{1,0:T(8,128)(2,1)S(1)}) custom-call(f32[16]{0:T(128)S(1)} %copy-done.8, f32[16]{0:T(128)S(1)} %copy-done.13, bf16[256,1024]{1,0:T(8,128)(2,1)S(1)} %copy-done.3, f32[16,256]{1,0:T(8,128)S(1)} %copy-done.4, bf16[16,256]{1,0:T(8,128)(2,1)S(1)} %copy-done.5, bf16[16,256]{1,0:T(8,128)(2,1)S(1)} %copy-done.6, ...), custom_call_target="tpu_custom_call" | custom-call | flops 2147483648 | bytes 3145728 | tf_op jit(solution)/shard_map/intra/pallas_call | solution.py:428
  26.3 5.5 %all-to-all-done.1.rows_ref = bf16[8,16,1152]{2,1,0:T(8,128)(2,1)S(1)} async-done(((bf16[8,16,1152]{2,1,0:T(8,128)(2,1)}), bf16[8,16,1152]{2,1,0:T(8,128)(2,1)S(1)}, u32[]{:S(2)}, u32[]{:S(2)}) %all-to-all-start.1) | async-done | bytes 294944 | tf_op jit(solution)/shard_map/all_to_all | solution.py:364
  31.8 2.6 %finish.1 = (bf16[256,1024]{1,0:T(8,128)(2,1)}, bf16[256,256]{1,0:T(8,128)(2,1)}) custom-call(s32[4]{0:T(128)S(1)} %pad_add_fusion.refs_0_.place_ref, bf16[8,16,1152]{2,1,0:T(8,128)(2,1)S(1)} %all-to-all-done.1.rows_ref, f32[16,1024]{1,0:T(8,128)S(1)} %get-tuple-element.13.refs_6_.before_ref, f32[16,1024]{1,0:T(8,128)S(1)} %get-tuple-element.14.decay_ref, ...), custom_call_target="tpu_custom_call" | custom-call | flops 536870912 | bytes 4194304 | tf_op jit(solution)/shard_map/finish/pallas_call | solution.py:437
  34.4 9.9 %all-to-all-start.2 = ((bf16[16,16,256]{2,1,0:T(8,128)(2,1)}), bf16[16,16,256]{2,1,0:T(8,128)(2,1)S(1)}, u32[]{:S(2)}, u32[]{:S(2)}) async-start(bf16[16,16,256]{2,1,0:T(8,128)(2,1)} %bitcast.5), calls=%async_computation.2 | async-start | bytes 262144 | tf_op jit(solution)/shard_map/all_to_all | solution.py:364
  44.4 8.7 %all-to-all-done.2.refs_0_ = bf16[16,16,256]{2,1,0:T(8,128)(2,1)S(1)} async-done(((bf16[16,16,256]{2,1,0:T(8,128)(2,1)}), bf16[16,16,256]{2,1,0:T(8,128)(2,1)S(1)}, u32[]{:S(2)}, u32[]{:S(2)}) %all-to-all-start.2) | async-done | bytes 131104 | tf_op jit(solution)/shard_map/all_to_all | solution.py:364
  54.0 6.9 %all-to-all-start.3 = ((bf16[64,16,256]{2,1,0:T(8,128)(2,1)}), bf16[64,16,256]{2,1,0:T(8,128)(2,1)S(1)}, u32[]{:S(2)}, u32[]{:S(2)}) async-start(bf16[64,16,256]{2,1,0:T(8,128)(2,1)} %sum.1.refs_1_.order_ref), calls=%async_computation.3 | async-start | bytes 1048576 | tf_op jit(solution)/shard_map/all_to_all | solution.py:364
  60.9 2.6 %collective-permute-start = (bf16[256,512]{1,0:T(8,128)(2,1)S(1)}, bf16[256,512]{1,0:T(8,128)(2,1)S(1)}, u32[]{:S(2)}, u32[]{:S(2)}) collective-permute-start(bf16[256,512]{1,0:T(8,128)(2,1)S(1)} %copy.18), channel_id=1, source_target_pairs={{0,16},{16,0},{32,48},{48,32},{1,17},{17,1},{33,49},{49,33},{2,18}... | collective-permute-start | bytes 786440 | tf_op jit(solution)/shard_map/ppermute | solution.py:360
  63.5 2.7 %collective-permute-start.1 = (bf16[256,512]{1,0:T(8,128)(2,1)S(1)}, bf16[256,512]{1,0:T(8,128)(2,1)S(1)}, u32[]{:S(2)}, u32[]{:S(2)}) collective-permute-start(bf16[256,512]{1,0:T(8,128)(2,1)S(1)} %copy.18), channel_id=1, source_target_pairs={{0,48},{16,32},{32,16},{48,0},{1,49},{17,33},{33,17},{49,1},{2,50}... | collective-permute-start | bytes 786440 | tf_op jit(solution)/shard_map/ppermute | solution.py:360
  66.9 4.8 %collective-permute-done.refs_3_.q_ref = bf16[256,512]{1,0:T(8,128)(2,1)S(1)} collective-permute-done((bf16[256,512]{1,0:T(8,128)(2,1)S(1)}, bf16[256,512]{1,0:T(8,128)(2,1)S(1)}, u32[]{:S(2)}, u32[]{:S(2)}) %collective-permute-start) | collective-permute-done | bytes 262176 | tf_op jit(solution)/shard_map/ppermute | solution.py:360
  71.7 3.4 %collective-permute-done.1.refs_4_.refs_1_ = bf16[256,512]{1,0:T(8,128)(2,1)S(1)} collective-permute-done((bf16[256,512]{1,0:T(8,128)(2,1)S(1)}, bf16[256,512]{1,0:T(8,128)(2,1)S(1)}, u32[]{:S(2)}, u32[]{:S(2)}) %collective-permute-start.1) | collective-permute-done | bytes 262176 | tf_op jit(solution)/shard_map/ppermute | solution.py:360
  75.1 6.4 %all-to-all-done.3 = bf16[64,16,256]{2,1,0:T(8,128)(2,1)S(1)} async-done(((bf16[64,16,256]{2,1,0:T(8,128)(2,1)}), bf16[64,16,256]{2,1,0:T(8,128)(2,1)S(1)}, u32[]{:S(2)}, u32[]{:S(2)}) %all-to-all-start.3) | async-done | bytes 524320 | tf_op jit(solution)/shard_map/all_to_all | solution.py:364
  84.3 3.1 %collective-permute-start.3 = (bf16[256,512]{1,0:T(8,128)(2,1)S(1)}, bf16[256,512]{1,0:T(8,128)(2,1)S(1)}, u32[]{:S(2)}, u32[]{:S(2)}) collective-permute-start(bf16[256,512]{1,0:T(8,128)(2,1)S(1)} %collective-permute-done.refs_3_.q_ref), channel_id=1, source_target_pairs={{0,48},{16,32},{32,16},{48,0},{1,49},{17,33},{33,17},{49,1},{2,50}... | collective-permute-start | bytes 786440 | tf_op jit(solution)/shard_map/ppermute | solution.py:360
  87.4 3.6 %attend.4 = (bf16[272,512]{1,0:T(8,128)(2,1)S(1)}, bf16[2048,256]{1,0:T(8,128)(2,1)S(1)}, bf16[2048,256]{1,0:T(8,128)(2,1)S(1)}) custom-call(s32[4]{0:T(128)S(1)} %pad_add_fusion.refs_0_.place_ref, bf16[256,512]{1,0:T(8,128)(2,1)S(1)} %collective-permute-done.refs_3_.q_ref, bf16[1024,256]{1,0:T(8,128)(2,1)S(1)} %rebuild.1.mine_ref, ...), custom_call_target="tpu_custom_call" | custom-call | flops 1073741824 | bytes 4194304 | tf_op jit(solution)/shard_map/attend/pallas_call | solution.py:499
  93.0 3.2 %collective-permute-done.3.refs_1_ = bf16[256,512]{1,0:T(8,128)(2,1)S(1)} collective-permute-done((bf16[256,512]{1,0:T(8,128)(2,1)S(1)}, bf16[256,512]{1,0:T(8,128)(2,1)S(1)}, u32[]{:S(2)}, u32[]{:S(2)}) %collective-permute-start.3) | collective-permute-done | bytes 262176 | tf_op jit(solution)/shard_map/ppermute | solution.py:360
  96.1 3.4 %attend.5.refs_4_ = bf16[272,512]{1,0:T(8,128)(2,1)S(1)} custom-call(s32[4]{0:T(128)S(1)} %pad_add_fusion.refs_0_.place_ref, bf16[256,512]{1,0:T(8,128)(2,1)S(1)} %collective-permute-done.3.refs_1_, bf16[2048,256]{1,0:T(8,128)(2,1)S(1)} %get-tuple-element.19.refs_2_, bf16[2048,256]{1,0:T(8,128)(2,1)S(1)} %get-tuple-element.20.refs_3_, ...), custom_call_target="tpu_custom_call" | custom-call | flops 1073741824 | bytes 4194304 | tf_op jit(solution)/shard_map/attend/pallas_call | solution.py:510
  99.5 2.5 %collective-permute-start.5 = (bf16[272,512]{1,0:T(8,128)(2,1)S(1)}, bf16[272,512]{1,0:T(8,128)(2,1)S(1)}, u32[]{:S(2)}, u32[]{:S(2)}) collective-permute-start(bf16[272,512]{1,0:T(8,128)(2,1)S(1)} %attend.5.refs_4_), channel_id=1, source_target_pairs={{0,32},{16,48},{32,0},{48,16},{1,33},{17,49},{33,1},{49,17},{2,34}... | collective-permute-start | bytes 835592 | tf_op jit(solution)/shard_map/ppermute | solution.py:360
  102.0 3.4 %attend.6.refs_4_ = bf16[272,512]{1,0:T(8,128)(2,1)S(1)} custom-call(s32[4]{0:T(128)S(1)} %pad_add_fusion.refs_0_.place_ref, bf16[256,512]{1,0:T(8,128)(2,1)S(1)} %collective-permute-done.1.refs_4_.refs_1_, bf16[2048,256]{1,0:T(8,128)(2,1)S(1)} %get-tuple-element.19.refs_2_, bf16[2048,256]{1,0:T(8,128)(2,1)S(1)} %get-tuple-element.20.refs_3_, ...), custom_call_target="tpu_custom_call" | custom-call | flops 1073741824 | bytes 4194304 | tf_op jit(solution)/shard_map/attend/pallas_call | solution.py:510
  105.3 3.7 %collective-permute-start.6 = (bf16[272,512]{1,0:T(8,128)(2,1)S(1)}, bf16[272,512]{1,0:T(8,128)(2,1)S(1)}, u32[]{:S(2)}, u32[]{:S(2)}) collective-permute-start(bf16[272,512]{1,0:T(8,128)(2,1)S(1)} %attend.6.refs_4_), channel_id=1, source_target_pairs={{0,48},{16,32},{32,16},{48,0},{1,49},{17,33},{33,17},{49,1},{2,50}... | collective-permute-start | bytes 835592 | tf_op jit(solution)/shard_map/ppermute | solution.py:360
  109.1 3.4 %attend.7.own_ref = bf16[272,512]{1,0:T(8,128)(2,1)S(1)} custom-call(s32[4]{0:T(128)S(1)} %pad_add_fusion.refs_0_.place_ref, bf16[256,512]{1,0:T(8,128)(2,1)S(1)} %copy-done, bf16[2048,256]{1,0:T(8,128)(2,1)S(1)} %get-tuple-element.19.refs_2_, bf16[2048,256]{1,0:T(8,128)(2,1)S(1)} %get-tuple-element.20.refs_3_, bf16[272,512]{1,0:T(8,128)(2,1)S(1)} %attend.6.refs_4_), custom_call_target="tpu_custom_call" | custom-call | flops 1073741824 | bytes 4194304 | tf_op jit(solution)/shard_map/attend/pallas_call | solution.py:510
  112.4 4.7 %collective-permute-done.6.back3_ref = bf16[272,512]{1,0:T(8,128)(2,1)S(1)} collective-permute-done((bf16[272,512]{1,0:T(8,128)(2,1)S(1)}, bf16[272,512]{1,0:T(8,128)(2,1)S(1)}, u32[]{:S(2)}, u32[]{:S(2)}) %collective-permute-start.6) | collective-permute-done | bytes 278560 | tf_op jit(solution)/shard_map/ppermute | solution.py:360
  (42 shorter events, 10.1 us)
Async XLA Ops:
  0.6 7.0 %copy-start.11 = (bf16[256,512]{1,0:T(8,128)(2,1)S(1)}, bf16[256,512]{1,0:T(8,128)(2,1)}, u32[]{:S(2)}) copy-start(bf16[256,512]{1,0:T(8,128)(2,1)} %refs_0_.4) | copy-start | bytes 786436
  0.6 7.0 %copy-start.12 = (bf16[512,256]{1,0:T(8,128)(2,1)S(1)}, bf16[512,256]{1,0:T(8,128)(2,1)}, u32[]{:S(2)}) copy-start(bf16[512,256]{1,0:T(8,128)(2,1)} %refs_1_.3) | copy-start | bytes 786436
  3.2 4.4 %copy-start.1 = (bf16[4,16,1152]{2,1,0:T(8,128)(2,1)S(1)}, bf16[4,16,1152]{2,1,0:T(8,128)(2,1)}, u32[]{:S(2)}) copy-start(bf16[4,16,1152]{2,1,0:T(8,128)(2,1)} %state.1.refs_2_) | copy-start | bytes 442372
  3.2 10.5 %all-to-all-start = ((bf16[4,16,1152]{2,1,0:T(8,128)(2,1)}), bf16[4,16,1152]{2,1,0:T(8,128)(2,1)S(1)}, u32[]{:S(2)}, u32[]{:S(2)}) async-start(bf16[4,16,1152]{2,1,0:T(8,128)(2,1)} %state.1.refs_2_), calls=%async_computation | async-start | bytes 294912 | tf_op jit(solution)/shard_map/all_to_all | solution.py:364
  7.9 15.5 %copy-start.3 = (bf16[256,1024]{1,0:T(8,128)(2,1)S(1)}, bf16[256,1024]{1,0:T(8,128)(2,1)}, u32[]{:S(2)}) copy-start(bf16[256,1024]{1,0:T(8,128)(2,1)} %refs_2_.1) | copy-start | bytes 1572868
  15.2 8.2 %copy-start.4 = (f32[16,256]{1,0:T(8,128)S(1)}, f32[16,256]{1,0:T(8,128)}, u32[]{:S(2)}) copy-start(f32[16,256]{1,0:T(8,128)} %refs_3_.1) | copy-start | bytes 49156
  15.2 8.2 %copy-start.5 = (bf16[16,256]{1,0:T(8,128)(2,1)S(1)}, bf16[16,256]{1,0:T(8,128)(2,1)}, u32[]{:S(2)}) copy-start(bf16[16,256]{1,0:T(8,128)(2,1)} %refs_4_.1) | copy-start | bytes 24580
  15.2 8.2 %copy-start.6 = (bf16[16,256]{1,0:T(8,128)(2,1)S(1)}, bf16[16,256]{1,0:T(8,128)(2,1)}, u32[]{:S(2)}) copy-start(bf16[16,256]{1,0:T(8,128)(2,1)} %c_ref.1) | copy-start | bytes 24580
  15.2 16.6 %all-to-all-start.1 = ((bf16[8,16,1152]{2,1,0:T(8,128)(2,1)}), bf16[8,16,1152]{2,1,0:T(8,128)(2,1)S(1)}, u32[]{:S(2)}, u32[]{:S(2)}) async-start(bf16[8,16,1152]{2,1,0:T(8,128)(2,1)} %get-tuple-element.12), calls=%async_computation.1 | async-start | bytes 589824 | tf_op jit(solution)/shard_map/all_to_all | solution.py:364
  23.4 0.7 copy-start.13
  24.0 7.8 %copy-start.2 = (bf16[1024,256]{1,0:T(8,128)(2,1)S(1)}, bf16[1024,256]{1,0:T(8,128)(2,1)}, u32[]{:S(2)}) copy-start(bf16[1024,256]{1,0:T(8,128)(2,1)} %w_ref.1) | copy-start | bytes 1572868
  26.3 5.5 %copy-start.7 = (f32[1024]{0:T(1024)S(1)}, f32[1024]{0:T(1024)}, u32[]{:S(2)}) copy-start(f32[1024]{0:T(1024)} %param.20) | copy-start | bytes 12292
  34.4 9.9 %copy-start = (bf16[256,512]{1,0:T(8,128)(2,1)S(1)}, bf16[256,512]{1,0:T(8,128)(2,1)}, u32[]{:S(2)}) copy-start(bf16[256,512]{1,0:T(8,128)(2,1)} %refs_1_.5) | copy-start | bytes 786436
  34.4 18.7 %all-to-all-start.2 = ((bf16[16,16,256]{2,1,0:T(8,128)(2,1)}), bf16[16,16,256]{2,1,0:T(8,128)(2,1)S(1)}, u32[]{:S(2)}, u32[]{:S(2)}) async-start(bf16[16,16,256]{2,1,0:T(8,128)(2,1)} %bitcast.5), calls=%async_computation.2 | async-start | bytes 262144 | tf_op jit(solution)/shard_map/all_to_all | solution.py:364
  54.0 27.6 %all-to-all-start.3 = ((bf16[64,16,256]{2,1,0:T(8,128)(2,1)}), bf16[64,16,256]{2,1,0:T(8,128)(2,1)S(1)}, u32[]{:S(2)}, u32[]{:S(2)}) async-start(bf16[64,16,256]{2,1,0:T(8,128)(2,1)} %sum.1.refs_1_.order_ref), calls=%async_computation.3 | async-start | bytes 1048576 | tf_op jit(solution)/shard_map/all_to_all | solution.py:364
  60.9 5.4 %copy-start.9 = (bf16[256,1024]{1,0:T(8,128)(2,1)S(1)}, bf16[256,1024]{1,0:T(8,128)(2,1)}, u32[]{:S(2)}) copy-start(bf16[256,1024]{1,0:T(8,128)(2,1)} %wk_ref.1) | copy-start | bytes 1572868
  60.9 5.4 %copy-start.10 = (bf16[256,1024]{1,0:T(8,128)(2,1)S(1)}, bf16[256,1024]{1,0:T(8,128)(2,1)}, u32[]{:S(2)}) copy-start(bf16[256,1024]{1,0:T(8,128)(2,1)} %wv_ref.1) | copy-start | bytes 1572868
  60.9 10.8 %collective-permute-start = (bf16[256,512]{1,0:T(8,128)(2,1)S(1)}, bf16[256,512]{1,0:T(8,128)(2,1)S(1)}, u32[]{:S(2)}, u32[]{:S(2)}) collective-permute-start(bf16[256,512]{1,0:T(8,128)(2,1)S(1)} %copy.18), channel_id=1, source_target_pairs={{0,16},{16,0},{32,48},{48,32},{1,17},{17,1},{33,49},{49,33},{2,18}... | collective-permute-start | bytes 786440 | tf_op jit(solution)/shard_map/ppermute | solution.py:360
  63.5 11.6 %collective-permute-start.1 = (bf16[256,512]{1,0:T(8,128)(2,1)S(1)}, bf16[256,512]{1,0:T(8,128)(2,1)S(1)}, u32[]{:S(2)}, u32[]{:S(2)}) collective-permute-start(bf16[256,512]{1,0:T(8,128)(2,1)S(1)} %copy.18), channel_id=1, source_target_pairs={{0,48},{16,32},{32,16},{48,0},{1,49},{17,33},{33,17},{49,1},{2,50}... | collective-permute-start | bytes 786440 | tf_op jit(solution)/shard_map/ppermute | solution.py:360
  82.4 5.0 %collective-permute-start.2 = (bf16[1024,256]{1,0:T(8,128)(2,1)S(1)}, bf16[1024,256]{1,0:T(8,128)(2,1)S(1)}, u32[]{:S(2)}, u32[]{:S(2)}) collective-permute-start(bf16[1024,256]{1,0:T(8,128)(2,1)S(1)} %rebuild.1.mine_ref), channel_id=1, source_target_pairs={{0,1},{1,0},{2,3},{3,2},{4,5},{5,4},{6,7},{7,6},{8,9},{9,8},{10,11... | collective-permute-start | bytes 1572872 | tf_op jit(solution)/shard_map/ppermute | solution.py:360
  84.3 11.8 %collective-permute-start.3 = (bf16[256,512]{1,0:T(8,128)(2,1)S(1)}, bf16[256,512]{1,0:T(8,128)(2,1)S(1)}, u32[]{:S(2)}, u32[]{:S(2)}) collective-permute-start(bf16[256,512]{1,0:T(8,128)(2,1)S(1)} %collective-permute-done.refs_3_.q_ref), channel_id=1, source_target_pairs={{0,48},{16,32},{32,16},{48,0},{1,49},{17,33},{33,17},{49,1},{2,50}... | collective-permute-start | bytes 786440 | tf_op jit(solution)/shard_map/ppermute | solution.py:360
  91.0 10.9 %collective-permute-start.4 = (bf16[272,512]{1,0:T(8,128)(2,1)S(1)}, bf16[272,512]{1,0:T(8,128)(2,1)S(1)}, u32[]{:S(2)}, u32[]{:S(2)}) collective-permute-start(bf16[272,512]{1,0:T(8,128)(2,1)S(1)} %get-tuple-element.21.refs_4_), channel_id=1, source_target_pairs={{0,16},{16,0},{32,48},{48,32},{1,17},{17,1},{33,49},{49,33},{2,18}... | collective-permute-start | bytes 835592 | tf_op jit(solution)/shard_map/ppermute | solution.py:360
  99.5 12.9 %collective-permute-start.5 = (bf16[272,512]{1,0:T(8,128)(2,1)S(1)}, bf16[272,512]{1,0:T(8,128)(2,1)S(1)}, u32[]{:S(2)}, u32[]{:S(2)}) collective-permute-start(bf16[272,512]{1,0:T(8,128)(2,1)S(1)} %attend.5.refs_4_), channel_id=1, source_target_pairs={{0,32},{16,48},{32,0},{48,16},{1,33},{17,49},{33,1},{49,17},{2,34}... | collective-permute-start | bytes 835592 | tf_op jit(solution)/shard_map/ppermute | solution.py:360
  105.3 11.8 %collective-permute-start.6 = (bf16[272,512]{1,0:T(8,128)(2,1)S(1)}, bf16[272,512]{1,0:T(8,128)(2,1)S(1)}, u32[]{:S(2)}, u32[]{:S(2)}) collective-permute-start(bf16[272,512]{1,0:T(8,128)(2,1)S(1)} %attend.6.refs_4_), channel_id=1, source_target_pairs={{0,48},{16,32},{32,16},{48,0},{1,49},{17,33},{33,17},{49,1},{2,50}... | collective-permute-start | bytes 835592 | tf_op jit(solution)/shard_map/ppermute | solution.py:360
  (1 other events, 0.7 us)

commit v4 on v2

--- a/solution.py
+++ b/solution.py
@@ -244,22 +244,31 @@
             out = slice((part * NY + block) * HALF, (part * NY + block + 1) * HALF)
             bias = jnp.where(y >= block, 0.0, NEG_BIG)
             k_ref[out, :HD] = ref[rows, :HD]
-            k_ref[out, HD:] = jnp.where(lane == 0, bias, 0.0).astype(BF16)
+            near = 1.0 if block == 0 else 0.0
+            k_ref[out, HD:] = jnp.where(
+                lane == 0, bias, jnp.where(lane == 1, near, 0.0)
+            ).astype(BF16)
             v_ref[out, :HD] = ref[rows, HD:]
             v_ref[out, HD:] = ones
 
 
+def own_masked(scores, core):
+    token = iota((2 * ROWS, HALF), 0) & (ROWS - 1)
+    slot = iota((2 * ROWS, HALF), 1)
+    pieces = []
+    for part, own in enumerate((core, 1 - core)):
+        key = (slot // PIECE) * (2 * PIECE) + own * PIECE + (slot & (PIECE - 1))
+        begin = part * NY * HALF
+        pieces.append(jnp.where(key <= token, scores[:, begin : begin + HALF], NEG_BIG))
+        pieces.append(scores[:, begin + HALF : begin + NY * HALF])
+    return jnp.concatenate(pieces, axis=1)
+
+
 def attend_kernel(step, place_ref, q_ref, k_ref, v_ref, out_ref):
     x, core = place_ref[1], place_ref[3]
-    ahead = ((x ^ step) - x) * ROWS
     lane = iota((ROWS, 128), 1)
-    unit = jnp.where(lane == 0, 1.0, 0.0).astype(BF16)
-    token = iota((ROWS, HALF), 0) + ahead
-    slot = iota((ROWS, HALF), 1)
-    allowed = []
-    for own in (core, 1 - core):
-        key = (slot // PIECE) * (2 * PIECE) + own * PIECE + (slot & (PIECE - 1))
-        allowed.append(key <= token)
+    behind = jnp.where((x ^ step) < x, NEG_BIG, 0.0)
+    unit = jnp.where(lane == 0, 1.0, jnp.where(lane == 1, behind, 0.0)).astype(BF16)
 
     def scored(first):
         query = jnp.concatenate(
@@ -273,19 +282,14 @@
             query, k_ref[...], (((1,), (1,)), ((), ())), preferred_element_type=F32
         )
 
-    allowed = [jnp.concatenate([part, part], axis=0) for part in allowed]
     stats = jnp.zeros((ROWS, 128), F32)
     following = scored(0)
     for first in range(0, HEADS_Q, 2):
         scores = following
         if first + 2 < HEADS_Q:
             following = scored(first + 2)
-        pieces = []
-        for part in range(2):
-            begin = part * NY * HALF
-            pieces.append(jnp.where(allowed[part], scores[:, begin : begin + HALF], NEG_BIG))
-            pieces.append(scores[:, begin + HALF : begin + NY * HALF])
-        scores = jnp.concatenate(pieces, axis=1)
+        if step == 0:
+            scores = own_masked(scores, core)
         best = jnp.max(scores, axis=1, keepdims=True)
         weights = jnp.exp2(scores - best).astype(BF16)
         sums = dot(weights, v_ref[...])
@@ -466,9 +470,7 @@
 
     blocks = exchange(latents, ("y", "z")).reshape(NY, HALF, RANK)
     lent = copied(latents)
-    visiting1 = swap(lent, "x", NX, 1)
-    visiting3 = swap(lent, "x", NX, 3)
-    visiting2 = swap(visiting1, "x", NX, 3)
+    visiting1, visiting2, visiting3 = [swap(lent, "x", NX, k) for k in (1, 2, 3)]
     weights = pl.pallas_call(
         weights_kernel,
         out_shape=shape((RANK, 2 * HD), BF16),

time: 116 us -> 115 us (level)
  the two profiles are of different devices: /device:TPU:2 before, /device:TPU:16 now
where the time goes in v4:
time: 115 us; the launch traced here: 114 us
  starting transfers between devices  51.3 us (45%)
  waiting for transfers between devices  36 us (31%)
  Pallas kernels  25.5 us (22%)
    all_to_all x4, starting transfers between devices, exchange(): return lax.all_to_all(chunks, axes, 0, 0, tiled=True)  29.4 us
    ppermute x7, starting transfers between devices, swap(): return lax.ppermute(value, axis, [(i, i ^ step) for i in range(size)])  21.9 us
    all_to_all x4, waiting for transfers between devices, exchange(): return lax.all_to_all(chunks, axes, 0, 0, tiled=True)  19.9 us
    ppermute x7, waiting for transfers between devices, swap(): return lax.ppermute(value, axis, [(i, i ^ step) for i in range(size)])  16 us
    pallas_call x3, Pallas kernels, body(): call(after(kernel, 4), 'attend', answer, [SM, VM, VM, VM] + [ANY] * (len(...  9.26 us
    pallas_call x1, Pallas kernels, body(): call(functools.partial(attend_first_kernel, 2), 'attend', (answer, wide,...  3.27 us
    pallas_call x1, Pallas kernels, body(): call(finish_kernel, 'finish', (shape((ROWS, INNER), BF16), shape((ROWS, R...  2.61 us
    pallas_call x1, Pallas kernels, body(): call(state_kernel, 'state', shape((NX, STATE, PAY), BF16), [SM, (ROWS, IN...  2.59 us
  transfers between devices with their start and end apart: 11, of which 9 were waited for; matrix products, arithmetic and copies ran while one was open for 0% of the time, Pallas kernels for 11%

profile of v4, /device:TPU:16, one launch (start us, length us, event | category | flops | bytes accessed | tf_op | source)
XLA Modules:
  0.0 114.3 jit_solution(17070095473914470694)
XLA Ops:
  0.6 2.6 %state.1.refs_2_ = bf16[4,16,1152]{2,1,0:T(8,128)(2,1)} custom-call(f32[16]{0:T(128)} %refs_0_.5, bf16[256,1024]{1,0:T(8,128)(2,1)} %refs_2_.1, f32[16,256]{1,0:T(8,128)} %refs_3_.1, bf16[16,256]{1,0:T(8,128)(2,1)} %refs_4_.1), custom_call_target="tpu_custom_call" | custom-call | flops 134217728 | bytes 1048576 | tf_op jit(solution)/shard_map/state/pallas_call | solution.py:397
  3.2 4.4 %all-to-all-start = ((bf16[4,16,1152]{2,1,0:T(8,128)(2,1)}), bf16[4,16,1152]{2,1,0:T(8,128)(2,1)S(1)}, u32[]{:S(2)}, u32[]{:S(2)}) async-start(bf16[4,16,1152]{2,1,0:T(8,128)(2,1)} %state.1.refs_2_), calls=%async_computation | async-start | bytes 294912 | tf_op jit(solution)/shard_map/all_to_all | solution.py:368
  8.0 5.7 %all-to-all-done.refs_1_ = bf16[4,16,1152]{2,1,0:T(8,128)(2,1)S(1)} async-done(((bf16[4,16,1152]{2,1,0:T(8,128)(2,1)}), bf16[4,16,1152]{2,1,0:T(8,128)(2,1)S(1)}, u32[]{:S(2)}, u32[]{:S(2)}) %all-to-all-start) | async-done | bytes 147488 | tf_op jit(solution)/shard_map/all_to_all | solution.py:368
  15.2 8.2 %all-to-all-start.1 = ((bf16[8,16,1152]{2,1,0:T(8,128)(2,1)}), bf16[8,16,1152]{2,1,0:T(8,128)(2,1)S(1)}, u32[]{:S(2)}, u32[]{:S(2)}) async-start(bf16[8,16,1152]{2,1,0:T(8,128)(2,1)} %get-tuple-element.12), calls=%async_computation.1 | async-start | bytes 589824 | tf_op jit(solution)/shard_map/all_to_all | solution.py:368
  24.0 2.2 %intra.1 = (f32[256,1024]{1,0:T(8,128)S(1)}, bf16[256,128]{1,0:T(8,128)(2,1)S(1)}) custom-call(f32[16]{0:T(128)S(1)} %copy-done.8, f32[16]{0:T(128)S(1)} %copy-done.13, bf16[256,1024]{1,0:T(8,128)(2,1)S(1)} %copy-done.3, f32[16,256]{1,0:T(8,128)S(1)} %copy-done.4, bf16[16,256]{1,0:T(8,128)(2,1)S(1)} %copy-done.5, bf16[16,256]{1,0:T(8,128)(2,1)S(1)} %copy-done.6, ...), custom_call_target="tpu_custom_call" | custom-call | flops 2147483648 | bytes 3145728 | tf_op jit(solution)/shard_map/intra/pallas_call | solution.py:432
  26.3 5.5 %all-to-all-done.1.rows_ref = bf16[8,16,1152]{2,1,0:T(8,128)(2,1)S(1)} async-done(((bf16[8,16,1152]{2,1,0:T(8,128)(2,1)}), bf16[8,16,1152]{2,1,0:T(8,128)(2,1)S(1)}, u32[]{:S(2)}, u32[]{:S(2)}) %all-to-all-start.1) | async-done | bytes 294944 | tf_op jit(solution)/shard_map/all_to_all | solution.py:368
  31.8 2.6 %finish.1 = (bf16[256,1024]{1,0:T(8,128)(2,1)}, bf16[256,256]{1,0:T(8,128)(2,1)}) custom-call(s32[4]{0:T(128)S(1)} %pad_add_fusion.refs_0_.place_ref, bf16[8,16,1152]{2,1,0:T(8,128)(2,1)S(1)} %all-to-all-done.1.rows_ref, f32[16,1024]{1,0:T(8,128)S(1)} %get-tuple-element.13.refs_6_.before_ref, f32[16,1024]{1,0:T(8,128)S(1)} %get-tuple-element.14.decay_ref, ...), custom_call_target="tpu_custom_call" | custom-call | flops 536870912 | bytes 4194304 | tf_op jit(solution)/shard_map/finish/pallas_call | solution.py:441
  34.4 9.9 %all-to-all-start.2 = ((bf16[16,16,256]{2,1,0:T(8,128)(2,1)}), bf16[16,16,256]{2,1,0:T(8,128)(2,1)S(1)}, u32[]{:S(2)}, u32[]{:S(2)}) async-start(bf16[16,16,256]{2,1,0:T(8,128)(2,1)} %bitcast.5), calls=%async_computation.2 | async-start | bytes 262144 | tf_op jit(solution)/shard_map/all_to_all | solution.py:368
  44.4 8.7 %all-to-all-done.2.refs_0_ = bf16[16,16,256]{2,1,0:T(8,128)(2,1)S(1)} async-done(((bf16[16,16,256]{2,1,0:T(8,128)(2,1)}), bf16[16,16,256]{2,1,0:T(8,128)(2,1)S(1)}, u32[]{:S(2)}, u32[]{:S(2)}) %all-to-all-start.2) | async-done | bytes 131104 | tf_op jit(solution)/shard_map/all_to_all | solution.py:368
  54.0 6.9 %all-to-all-start.3 = ((bf16[64,16,256]{2,1,0:T(8,128)(2,1)}), bf16[64,16,256]{2,1,0:T(8,128)(2,1)S(1)}, u32[]{:S(2)}, u32[]{:S(2)}) async-start(bf16[64,16,256]{2,1,0:T(8,128)(2,1)} %sum.1.refs_1_.order_ref), calls=%async_computation.3 | async-start | bytes 1048576 | tf_op jit(solution)/shard_map/all_to_all | solution.py:368
  60.9 3.2 %collective-permute-start.2 = (bf16[256,512]{1,0:T(8,128)(2,1)S(1)}, bf16[256,512]{1,0:T(8,128)(2,1)S(1)}, u32[]{:S(2)}, u32[]{:S(2)}) collective-permute-start(bf16[256,512]{1,0:T(8,128)(2,1)S(1)} %copy.18), channel_id=1, source_target_pairs={{0,48},{16,32},{32,16},{48,0},{1,49},{17,33},{33,17},{49,1},{2,50}... | collective-permute-start | bytes 786440 | tf_op jit(solution)/shard_map/ppermute | solution.py:364
  64.1 1.9 %collective-permute-start.1 = (bf16[256,512]{1,0:T(8,128)(2,1)S(1)}, bf16[256,512]{1,0:T(8,128)(2,1)S(1)}, u32[]{:S(2)}, u32[]{:S(2)}) collective-permute-start(bf16[256,512]{1,0:T(8,128)(2,1)S(1)} %copy.18), channel_id=1, source_target_pairs={{0,16},{16,0},{32,48},{48,32},{1,17},{17,1},{33,49},{49,33},{2,18}... | collective-permute-start | bytes 786440 | tf_op jit(solution)/shard_map/ppermute | solution.py:364
  66.1 5.4 %collective-permute-start = (bf16[256,512]{1,0:T(8,128)(2,1)S(1)}, bf16[256,512]{1,0:T(8,128)(2,1)S(1)}, u32[]{:S(2)}, u32[]{:S(2)}) collective-permute-start(bf16[256,512]{1,0:T(8,128)(2,1)S(1)} %copy.18), channel_id=1, source_target_pairs={{0,32},{16,48},{32,0},{48,16},{1,33},{17,49},{33,1},{49,17},{2,34}... | collective-permute-start | bytes 786440 | tf_op jit(solution)/shard_map/ppermute | solution.py:364
  72.9 2.2 %collective-permute-done.1.refs_3_.refs_1_ = bf16[256,512]{1,0:T(8,128)(2,1)S(1)} collective-permute-done((bf16[256,512]{1,0:T(8,128)(2,1)S(1)}, bf16[256,512]{1,0:T(8,128)(2,1)S(1)}, u32[]{:S(2)}, u32[]{:S(2)}) %collective-permute-start.1) | collective-permute-done | bytes 262176 | tf_op jit(solution)/shard_map/ppermute | solution.py:364
  75.2 6.5 %collective-permute-done.refs_4_.q_ref = bf16[256,512]{1,0:T(8,128)(2,1)S(1)} collective-permute-done((bf16[256,512]{1,0:T(8,128)(2,1)S(1)}, bf16[256,512]{1,0:T(8,128)(2,1)S(1)}, u32[]{:S(2)}, u32[]{:S(2)}) %collective-permute-start) | collective-permute-done | bytes 262176 | tf_op jit(solution)/shard_map/ppermute | solution.py:364
  82.5 1.9 %collective-permute-start.3 = (bf16[1024,256]{1,0:T(8,128)(2,1)S(1)}, bf16[1024,256]{1,0:T(8,128)(2,1)S(1)}, u32[]{:S(2)}, u32[]{:S(2)}) collective-permute-start(bf16[1024,256]{1,0:T(8,128)(2,1)S(1)} %rebuild.1.mine_ref), channel_id=1, source_target_pairs={{0,1},{1,0},{2,3},{3,2},{4,5},{5,4},{6,7},{7,6},{8,9},{9,8},{10,11... | collective-permute-start | bytes 1572872 | tf_op jit(solution)/shard_map/ppermute | solution.py:364
  86.3 3.3 %attend.4 = (bf16[272,512]{1,0:T(8,128)(2,1)S(1)}, bf16[2048,256]{1,0:T(8,128)(2,1)S(1)}, bf16[2048,256]{1,0:T(8,128)(2,1)S(1)}) custom-call(s32[4]{0:T(128)S(1)} %pad_add_fusion.refs_0_.place_ref, bf16[256,512]{1,0:T(8,128)(2,1)S(1)} %collective-permute-done.refs_4_.q_ref, bf16[1024,256]{1,0:T(8,128)(2,1)S(1)} %rebuild.1.mine_ref, ...), custom_call_target="tpu_custom_call" | custom-call | flops 1073741824 | bytes 4194304 | tf_op jit(solution)/shard_map/attend/pallas_call | solution.py:501
  89.6 2.8 %collective-permute-start.4 = (bf16[272,512]{1,0:T(8,128)(2,1)S(1)}, bf16[272,512]{1,0:T(8,128)(2,1)S(1)}, u32[]{:S(2)}, u32[]{:S(2)}) collective-permute-start(bf16[272,512]{1,0:T(8,128)(2,1)S(1)} %get-tuple-element.21.refs_4_), channel_id=1, source_target_pairs={{0,32},{16,48},{32,0},{48,16},{1,33},{17,49},{33,1},{49,17},{2,34}... | collective-permute-start | bytes 835592 | tf_op jit(solution)/shard_map/ppermute | solution.py:364
  92.3 3.1 %attend.5.refs_4_ = bf16[272,512]{1,0:T(8,128)(2,1)S(1)} custom-call(s32[4]{0:T(128)S(1)} %pad_add_fusion.refs_0_.place_ref, bf16[256,512]{1,0:T(8,128)(2,1)S(1)} %collective-permute-done.1.refs_3_.refs_1_, bf16[2048,256]{1,0:T(8,128)(2,1)S(1)} %get-tuple-element.19.refs_2_, bf16[2048,256]{1,0:T(8,128)(2,1)S(1)} %get-tuple-element.20.refs_3_, ...), custom_call_target="tpu_custom_call" | custom-call | flops 1073741824 | bytes 4194304 | tf_op jit(solution)/shard_map/attend/pallas_call | solution.py:512
  95.4 3.1 %attend.6.refs_4_ = bf16[272,512]{1,0:T(8,128)(2,1)S(1)} custom-call(s32[4]{0:T(128)S(1)} %pad_add_fusion.refs_0_.place_ref, bf16[256,512]{1,0:T(8,128)(2,1)S(1)} %collective-permute-done.2.refs_5_.refs_1_, bf16[2048,256]{1,0:T(8,128)(2,1)S(1)} %get-tuple-element.19.refs_2_, bf16[2048,256]{1,0:T(8,128)(2,1)S(1)} %get-tuple-element.20.refs_3_, ...), custom_call_target="tpu_custom_call" | custom-call | flops 1073741824 | bytes 4194304 | tf_op jit(solution)/shard_map/attend/pallas_call | solution.py:512
  98.5 4.4 %collective-permute-start.6 = (bf16[272,512]{1,0:T(8,128)(2,1)S(1)}, bf16[272,512]{1,0:T(8,128)(2,1)S(1)}, u32[]{:S(2)}, u32[]{:S(2)}) collective-permute-start(bf16[272,512]{1,0:T(8,128)(2,1)S(1)} %attend.6.refs_4_), channel_id=1, source_target_pairs={{0,48},{16,32},{32,16},{48,0},{1,49},{17,33},{33,17},{49,1},{2,50}... | collective-permute-start | bytes 835592 | tf_op jit(solution)/shard_map/ppermute | solution.py:364
  102.8 2.3 %collective-permute-start.5 = (bf16[272,512]{1,0:T(8,128)(2,1)S(1)}, bf16[272,512]{1,0:T(8,128)(2,1)S(1)}, u32[]{:S(2)}, u32[]{:S(2)}) collective-permute-start(bf16[272,512]{1,0:T(8,128)(2,1)S(1)} %attend.5.refs_4_), channel_id=1, source_target_pairs={{0,16},{16,0},{32,48},{48,32},{1,17},{17,1},{33,49},{49,33},{2,18}... | collective-permute-start | bytes 835592 | tf_op jit(solution)/shard_map/ppermute | solution.py:364
  105.1 3.1 %attend.7.own_ref = bf16[272,512]{1,0:T(8,128)(2,1)S(1)} custom-call(s32[4]{0:T(128)S(1)} %pad_add_fusion.refs_0_.place_ref, bf16[256,512]{1,0:T(8,128)(2,1)S(1)} %copy-done, bf16[2048,256]{1,0:T(8,128)(2,1)S(1)} %get-tuple-element.19.refs_2_, bf16[2048,256]{1,0:T(8,128)(2,1)S(1)} %get-tuple-element.20.refs_3_, bf16[272,512]{1,0:T(8,128)(2,1)S(1)} %attend.6.refs_4_, ...), custom_call_target="tpu_custom_call" | custom-call | flops 1073741824 | bytes 4194304 | tf_op jit(solution)/shard_map/attend/pallas_call | solution.py:512
  110.0 2.9 %collective-permute-done.5.back1_ref = bf16[272,512]{1,0:T(8,128)(2,1)S(1)} collective-permute-done((bf16[272,512]{1,0:T(8,128)(2,1)S(1)}, bf16[272,512]{1,0:T(8,128)(2,1)S(1)}, u32[]{:S(2)}, u32[]{:S(2)}) %collective-permute-start.5) | collective-permute-done | bytes 278560 | tf_op jit(solution)/shard_map/ppermute | solution.py:364
  (42 shorter events, 10.7 us)
Async XLA Ops:
  0.6 7.0 %copy-start.11 = (bf16[256,512]{1,0:T(8,128)(2,1)S(1)}, bf16[256,512]{1,0:T(8,128)(2,1)}, u32[]{:S(2)}) copy-start(bf16[256,512]{1,0:T(8,128)(2,1)} %refs_0_.4) | copy-start | bytes 786436
  0.6 7.0 %copy-start.12 = (bf16[512,256]{1,0:T(8,128)(2,1)S(1)}, bf16[512,256]{1,0:T(8,128)(2,1)}, u32[]{:S(2)}) copy-start(bf16[512,256]{1,0:T(8,128)(2,1)} %refs_1_.3) | copy-start | bytes 786436
  3.2 4.4 %copy-start.1 = (bf16[4,16,1152]{2,1,0:T(8,128)(2,1)S(1)}, bf16[4,16,1152]{2,1,0:T(8,128)(2,1)}, u32[]{:S(2)}) copy-start(bf16[4,16,1152]{2,1,0:T(8,128)(2,1)} %state.1.refs_2_) | copy-start | bytes 442372
  3.2 10.5 %all-to-all-start = ((bf16[4,16,1152]{2,1,0:T(8,128)(2,1)}), bf16[4,16,1152]{2,1,0:T(8,128)(2,1)S(1)}, u32[]{:S(2)}, u32[]{:S(2)}) async-start(bf16[4,16,1152]{2,1,0:T(8,128)(2,1)} %state.1.refs_2_), calls=%async_computation | async-start | bytes 294912 | tf_op jit(solution)/shard_map/all_to_all | solution.py:368
  7.9 15.5 %copy-start.3 = (bf16[256,1024]{1,0:T(8,128)(2,1)S(1)}, bf16[256,1024]{1,0:T(8,128)(2,1)}, u32[]{:S(2)}) copy-start(bf16[256,1024]{1,0:T(8,128)(2,1)} %refs_2_.1) | copy-start | bytes 1572868
  15.2 8.2 %copy-start.4 = (f32[16,256]{1,0:T(8,128)S(1)}, f32[16,256]{1,0:T(8,128)}, u32[]{:S(2)}) copy-start(f32[16,256]{1,0:T(8,128)} %refs_3_.1) | copy-start | bytes 49156
  15.2 8.2 %copy-start.5 = (bf16[16,256]{1,0:T(8,128)(2,1)S(1)}, bf16[16,256]{1,0:T(8,128)(2,1)}, u32[]{:S(2)}) copy-start(bf16[16,256]{1,0:T(8,128)(2,1)} %refs_4_.1) | copy-start | bytes 24580
  15.2 8.2 %copy-start.6 = (bf16[16,256]{1,0:T(8,128)(2,1)S(1)}, bf16[16,256]{1,0:T(8,128)(2,1)}, u32[]{:S(2)}) copy-start(bf16[16,256]{1,0:T(8,128)(2,1)} %c_ref.1) | copy-start | bytes 24580
  15.2 16.6 %all-to-all-start.1 = ((bf16[8,16,1152]{2,1,0:T(8,128)(2,1)}), bf16[8,16,1152]{2,1,0:T(8,128)(2,1)S(1)}, u32[]{:S(2)}, u32[]{:S(2)}) async-start(bf16[8,16,1152]{2,1,0:T(8,128)(2,1)} %get-tuple-element.12), calls=%async_computation.1 | async-start | bytes 589824 | tf_op jit(solution)/shard_map/all_to_all | solution.py:368
  23.4 0.7 copy-start.13
  24.0 7.8 %copy-start.2 = (bf16[1024,256]{1,0:T(8,128)(2,1)S(1)}, bf16[1024,256]{1,0:T(8,128)(2,1)}, u32[]{:S(2)}) copy-start(bf16[1024,256]{1,0:T(8,128)(2,1)} %w_ref.1) | copy-start | bytes 1572868
  26.3 5.5 %copy-start.7 = (f32[1024]{0:T(1024)S(1)}, f32[1024]{0:T(1024)}, u32[]{:S(2)}) copy-start(f32[1024]{0:T(1024)} %param.20) | copy-start | bytes 12292
  34.4 9.9 %copy-start = (bf16[256,512]{1,0:T(8,128)(2,1)S(1)}, bf16[256,512]{1,0:T(8,128)(2,1)}, u32[]{:S(2)}) copy-start(bf16[256,512]{1,0:T(8,128)(2,1)} %refs_1_.5) | copy-start | bytes 786436
  34.4 18.7 %all-to-all-start.2 = ((bf16[16,16,256]{2,1,0:T(8,128)(2,1)}), bf16[16,16,256]{2,1,0:T(8,128)(2,1)S(1)}, u32[]{:S(2)}, u32[]{:S(2)}) async-start(bf16[16,16,256]{2,1,0:T(8,128)(2,1)} %bitcast.5), calls=%async_computation.2 | async-start | bytes 262144 | tf_op jit(solution)/shard_map/all_to_all | solution.py:368
  54.0 27.7 %all-to-all-start.3 = ((bf16[64,16,256]{2,1,0:T(8,128)(2,1)}), bf16[64,16,256]{2,1,0:T(8,128)(2,1)S(1)}, u32[]{:S(2)}, u32[]{:S(2)}) async-start(bf16[64,16,256]{2,1,0:T(8,128)(2,1)} %sum.1.refs_1_.order_ref), calls=%async_computation.3 | async-start | bytes 1048576 | tf_op jit(solution)/shard_map/all_to_all | solution.py:368
  60.9 10.6 %copy-start.9 = (bf16[256,1024]{1,0:T(8,128)(2,1)S(1)}, bf16[256,1024]{1,0:T(8,128)(2,1)}, u32[]{:S(2)}) copy-start(bf16[256,1024]{1,0:T(8,128)(2,1)} %wk_ref.1) | copy-start | bytes 1572868
  60.9 10.6 %copy-start.10 = (bf16[256,1024]{1,0:T(8,128)(2,1)S(1)}, bf16[256,1024]{1,0:T(8,128)(2,1)}, u32[]{:S(2)}) copy-start(bf16[256,1024]{1,0:T(8,128)(2,1)} %wv_ref.1) | copy-start | bytes 1572868
  60.9 12.0 %collective-permute-start.2 = (bf16[256,512]{1,0:T(8,128)(2,1)S(1)}, bf16[256,512]{1,0:T(8,128)(2,1)S(1)}, u32[]{:S(2)}, u32[]{:S(2)}) collective-permute-start(bf16[256,512]{1,0:T(8,128)(2,1)S(1)} %copy.18), channel_id=1, source_target_pairs={{0,48},{16,32},{32,16},{48,0},{1,49},{17,33},{33,17},{49,1},{2,50}... | collective-permute-start | bytes 786440 | tf_op jit(solution)/shard_map/ppermute | solution.py:364
  64.1 11.0 %collective-permute-start.1 = (bf16[256,512]{1,0:T(8,128)(2,1)S(1)}, bf16[256,512]{1,0:T(8,128)(2,1)S(1)}, u32[]{:S(2)}, u32[]{:S(2)}) collective-permute-start(bf16[256,512]{1,0:T(8,128)(2,1)S(1)} %copy.18), channel_id=1, source_target_pairs={{0,16},{16,0},{32,48},{48,32},{1,17},{17,1},{33,49},{49,33},{2,18}... | collective-permute-start | bytes 786440 | tf_op jit(solution)/shard_map/ppermute | solution.py:364
  66.1 15.6 %collective-permute-start = (bf16[256,512]{1,0:T(8,128)(2,1)S(1)}, bf16[256,512]{1,0:T(8,128)(2,1)S(1)}, u32[]{:S(2)}, u32[]{:S(2)}) collective-permute-start(bf16[256,512]{1,0:T(8,128)(2,1)S(1)} %copy.18), channel_id=1, source_target_pairs={{0,32},{16,48},{32,0},{48,16},{1,33},{17,49},{33,1},{49,17},{2,34}... | collective-permute-start | bytes 786440 | tf_op jit(solution)/shard_map/ppermute | solution.py:364
  82.5 3.8 %collective-permute-start.3 = (bf16[1024,256]{1,0:T(8,128)(2,1)S(1)}, bf16[1024,256]{1,0:T(8,128)(2,1)S(1)}, u32[]{:S(2)}, u32[]{:S(2)}) collective-permute-start(bf16[1024,256]{1,0:T(8,128)(2,1)S(1)} %rebuild.1.mine_ref), channel_id=1, source_target_pairs={{0,1},{1,0},{2,3},{3,2},{4,5},{5,4},{6,7},{7,6},{8,9},{9,8},{10,11... | collective-permute-start | bytes 1572872 | tf_op jit(solution)/shard_map/ppermute | solution.py:364
  89.6 15.5 %collective-permute-start.4 = (bf16[272,512]{1,0:T(8,128)(2,1)S(1)}, bf16[272,512]{1,0:T(8,128)(2,1)S(1)}, u32[]{:S(2)}, u32[]{:S(2)}) collective-permute-start(bf16[272,512]{1,0:T(8,128)(2,1)S(1)} %get-tuple-element.21.refs_4_), channel_id=1, source_target_pairs={{0,32},{16,48},{32,0},{48,16},{1,33},{17,49},{33,1},{49,17},{2,34}... | collective-permute-start | bytes 835592 | tf_op jit(solution)/shard_map/ppermute | solution.py:364
  98.5 11.5 %collective-permute-start.6 = (bf16[272,512]{1,0:T(8,128)(2,1)S(1)}, bf16[272,512]{1,0:T(8,128)(2,1)S(1)}, u32[]{:S(2)}, u32[]{:S(2)}) collective-permute-start(bf16[272,512]{1,0:T(8,128)(2,1)S(1)} %attend.6.refs_4_), channel_id=1, source_target_pairs={{0,48},{16,32},{32,16},{48,0},{1,49},{17,33},{33,17},{49,1},{2,50}... | collective-permute-start | bytes 835592 | tf_op jit(solution)/shard_map/ppermute | solution.py:364
  102.8 10.0 %collective-permute-start.5 = (bf16[272,512]{1,0:T(8,128)(2,1)S(1)}, bf16[272,512]{1,0:T(8,128)(2,1)S(1)}, u32[]{:S(2)}, u32[]{:S(2)}) collective-permute-start(bf16[272,512]{1,0:T(8,128)(2,1)S(1)} %attend.5.refs_4_), channel_id=1, source_target_pairs={{0,16},{16,0},{32,48},{48,32},{1,17},{17,1},{33,49},{49,33},{2,18}... | collective-permute-start | bytes 835592 | tf_op jit(solution)/shard_map/ppermute | solution.py:364
  (1 other events, 0.7 us)

commit v5 on v4

--- a/solution.py
+++ b/solution.py
@@ -236,18 +236,18 @@
 
 
 def place_keys(y, mine_ref, other_ref, k_ref, v_ref):
-    lane = iota((HALF, HD), 1)
+    row = iota((HD, HALF), 0)
     ones = jnp.ones((HALF, HD), BF16)
     for part, ref in enumerate((mine_ref, other_ref)):
         for block in range(NY):
             rows = slice(block * HALF, (block + 1) * HALF)
             out = slice((part * NY + block) * HALF, (part * NY + block + 1) * HALF)
             bias = jnp.where(y >= block, 0.0, NEG_BIG)
-            k_ref[out, :HD] = ref[rows, :HD]
             near = 1.0 if block == 0 else 0.0
-            k_ref[out, HD:] = jnp.where(
-                lane == 0, bias, jnp.where(lane == 1, near, 0.0)
-            ).astype(BF16)
+            k_ref[:HD, out] = ref[rows, :HD].astype(F32).T.astype(BF16)
+            k_ref[HD:, out] = jnp.where(row == 0, bias, jnp.where(row == 1, near, 0.0)).astype(
+                BF16
+            )
             v_ref[out, :HD] = ref[rows, HD:]
             v_ref[out, HD:] = ones
 
@@ -278,9 +278,7 @@
             ],
             axis=0,
         )
-        return lax.dot_general(
-            query, k_ref[...], (((1,), (1,)), ((), ())), preferred_element_type=F32
-        )
+        return dot(query, k_ref[...])
 
     stats = jnp.zeros((ROWS, 128), F32)
     following = scored(0)
@@ -497,9 +495,9 @@
 
     work = 4 * ROWS * HEADS_Q * HD * NY * ROWS
     answer = shape((ROWS + 16, HEADS_Q * HD), BF16)
-    wide = shape((NY * ROWS, 2 * HD), BF16)
+    columns, wide = shape((2 * HD, NY * ROWS), BF16), shape((NY * ROWS, 2 * HD), BF16)
     done, keys, values = call(
-        functools.partial(attend_first_kernel, 2), "attend", (answer, wide, wide),
+        functools.partial(attend_first_kernel, 2), "attend", (answer, columns, wide),
         [SM, VM, VM, VM], 24, work, 4 * MIB,
     )(place, visiting2, mine, other)
     back = {2: swap(done, "x", NX, 2)}

time: 115 us -> 115 us (level)
  no operation moved by 1% of the time
where the time goes in v5:
time: 115 us; the launch traced here: 114 us
  starting transfers between devices  51.3 us (45%)
  waiting for transfers between devices  36 us (31%)
  Pallas kernels  25.5 us (22%)
    all_to_all x4, starting transfers between devices, exchange(): return lax.all_to_all(chunks, axes, 0, 0, tiled=True)  29.4 us
    ppermute x7, starting transfers between devices, swap(): return lax.ppermute(value, axis, [(i, i ^ step) for i in range(size)])  21.9 us
    all_to_all x4, waiting for transfers between devices, exchange(): return lax.all_to_all(chunks, axes, 0, 0, tiled=True)  19.9 us
    ppermute x7, waiting for transfers between devices, swap(): return lax.ppermute(value, axis, [(i, i ^ step) for i in range(size)])  16.1 us
    pallas_call x3, Pallas kernels, body(): call(after(kernel, 4), 'attend', answer, [SM, VM, VM, VM] + [ANY] * (len(...  9.17 us
    pallas_call x1, Pallas kernels, body(): call(functools.partial(attend_first_kernel, 2), 'attend', (answer, column...  3.37 us
    pallas_call x1, Pallas kernels, body(): call(finish_kernel, 'finish', (shape((ROWS, INNER), BF16), shape((ROWS, R...  2.61 us
    pallas_call x1, Pallas kernels, body(): call(state_kernel, 'state', shape((NX, STATE, PAY), BF16), [SM, (ROWS, IN...  2.59 us
  transfers between devices with their start and end apart: 11, of which 9 were waited for; matrix products, arithmetic and copies ran while one was open for 0% of the time, Pallas kernels for 11%

profile of v5, /device:TPU:16, one launch (start us, length us, event | category | flops | bytes accessed | tf_op | source)
XLA Modules:
  0.0 114.4 jit_solution(10553999454793262637)
XLA Ops:
  0.6 2.6 %state.1.refs_2_ = bf16[4,16,1152]{2,1,0:T(8,128)(2,1)} custom-call(f32[16]{0:T(128)} %refs_0_.5, bf16[256,1024]{1,0:T(8,128)(2,1)} %refs_2_.1, f32[16,256]{1,0:T(8,128)} %refs_3_.1, bf16[16,256]{1,0:T(8,128)(2,1)} %refs_4_.1), custom_call_target="tpu_custom_call" | custom-call | flops 134217728 | bytes 1048576 | tf_op jit(solution)/shard_map/state/pallas_call | solution.py:395
  3.2 4.4 %all-to-all-start = ((bf16[4,16,1152]{2,1,0:T(8,128)(2,1)}), bf16[4,16,1152]{2,1,0:T(8,128)(2,1)S(1)}, u32[]{:S(2)}, u32[]{:S(2)}) async-start(bf16[4,16,1152]{2,1,0:T(8,128)(2,1)} %state.1.refs_2_), calls=%async_computation | async-start | bytes 294912 | tf_op jit(solution)/shard_map/all_to_all | solution.py:366
  8.0 5.7 %all-to-all-done.refs_1_ = bf16[4,16,1152]{2,1,0:T(8,128)(2,1)S(1)} async-done(((bf16[4,16,1152]{2,1,0:T(8,128)(2,1)}), bf16[4,16,1152]{2,1,0:T(8,128)(2,1)S(1)}, u32[]{:S(2)}, u32[]{:S(2)}) %all-to-all-start) | async-done | bytes 147488 | tf_op jit(solution)/shard_map/all_to_all | solution.py:366
  15.2 8.2 %all-to-all-start.1 = ((bf16[8,16,1152]{2,1,0:T(8,128)(2,1)}), bf16[8,16,1152]{2,1,0:T(8,128)(2,1)S(1)}, u32[]{:S(2)}, u32[]{:S(2)}) async-start(bf16[8,16,1152]{2,1,0:T(8,128)(2,1)} %get-tuple-element.12), calls=%async_computation.1 | async-start | bytes 589824 | tf_op jit(solution)/shard_map/all_to_all | solution.py:366
  24.0 2.2 %intra.1 = (f32[256,1024]{1,0:T(8,128)S(1)}, bf16[256,128]{1,0:T(8,128)(2,1)S(1)}) custom-call(f32[16]{0:T(128)S(1)} %copy-done.8, f32[16]{0:T(128)S(1)} %copy-done.13, bf16[256,1024]{1,0:T(8,128)(2,1)S(1)} %copy-done.3, f32[16,256]{1,0:T(8,128)S(1)} %copy-done.4, bf16[16,256]{1,0:T(8,128)(2,1)S(1)} %copy-done.5, bf16[16,256]{1,0:T(8,128)(2,1)S(1)} %copy-done.6, ...), custom_call_target="tpu_custom_call" | custom-call | flops 2147483648 | bytes 3145728 | tf_op jit(solution)/shard_map/intra/pallas_call | solution.py:430
  26.3 5.5 %all-to-all-done.1.rows_ref = bf16[8,16,1152]{2,1,0:T(8,128)(2,1)S(1)} async-done(((bf16[8,16,1152]{2,1,0:T(8,128)(2,1)}), bf16[8,16,1152]{2,1,0:T(8,128)(2,1)S(1)}, u32[]{:S(2)}, u32[]{:S(2)}) %all-to-all-start.1) | async-done | bytes 294944 | tf_op jit(solution)/shard_map/all_to_all | solution.py:366
  31.8 2.6 %finish.1 = (bf16[256,1024]{1,0:T(8,128)(2,1)}, bf16[256,256]{1,0:T(8,128)(2,1)}) custom-call(s32[4]{0:T(128)S(1)} %pad_add_fusion.refs_0_.place_ref, bf16[8,16,1152]{2,1,0:T(8,128)(2,1)S(1)} %all-to-all-done.1.rows_ref, f32[16,1024]{1,0:T(8,128)S(1)} %get-tuple-element.13.refs_6_.before_ref, f32[16,1024]{1,0:T(8,128)S(1)} %get-tuple-element.14.decay_ref, ...), custom_call_target="tpu_custom_call" | custom-call | flops 536870912 | bytes 4194304 | tf_op jit(solution)/shard_map/finish/pallas_call | solution.py:439
  34.4 9.9 %all-to-all-start.2 = ((bf16[16,16,256]{2,1,0:T(8,128)(2,1)}), bf16[16,16,256]{2,1,0:T(8,128)(2,1)S(1)}, u32[]{:S(2)}, u32[]{:S(2)}) async-start(bf16[16,16,256]{2,1,0:T(8,128)(2,1)} %bitcast.5), calls=%async_computation.2 | async-start | bytes 262144 | tf_op jit(solution)/shard_map/all_to_all | solution.py:366
  44.4 8.7 %all-to-all-done.2.refs_0_ = bf16[16,16,256]{2,1,0:T(8,128)(2,1)S(1)} async-done(((bf16[16,16,256]{2,1,0:T(8,128)(2,1)}), bf16[16,16,256]{2,1,0:T(8,128)(2,1)S(1)}, u32[]{:S(2)}, u32[]{:S(2)}) %all-to-all-start.2) | async-done | bytes 131104 | tf_op jit(solution)/shard_map/all_to_all | solution.py:366
  54.0 6.9 %all-to-all-start.3 = ((bf16[64,16,256]{2,1,0:T(8,128)(2,1)}), bf16[64,16,256]{2,1,0:T(8,128)(2,1)S(1)}, u32[]{:S(2)}, u32[]{:S(2)}) async-start(bf16[64,16,256]{2,1,0:T(8,128)(2,1)} %sum.1.refs_1_.order_ref), calls=%async_computation.3 | async-start | bytes 1048576 | tf_op jit(solution)/shard_map/all_to_all | solution.py:366
  60.9 3.2 %collective-permute-start.2 = (bf16[256,512]{1,0:T(8,128)(2,1)S(1)}, bf16[256,512]{1,0:T(8,128)(2,1)S(1)}, u32[]{:S(2)}, u32[]{:S(2)}) collective-permute-start(bf16[256,512]{1,0:T(8,128)(2,1)S(1)} %copy.18), channel_id=1, source_target_pairs={{0,48},{16,32},{32,16},{48,0},{1,49},{17,33},{33,17},{49,1},{2,50}... | collective-permute-start | bytes 786440 | tf_op jit(solution)/shard_map/ppermute | solution.py:362
  64.1 1.9 %collective-permute-start.1 = (bf16[256,512]{1,0:T(8,128)(2,1)S(1)}, bf16[256,512]{1,0:T(8,128)(2,1)S(1)}, u32[]{:S(2)}, u32[]{:S(2)}) collective-permute-start(bf16[256,512]{1,0:T(8,128)(2,1)S(1)} %copy.18), channel_id=1, source_target_pairs={{0,16},{16,0},{32,48},{48,32},{1,17},{17,1},{33,49},{49,33},{2,18}... | collective-permute-start | bytes 786440 | tf_op jit(solution)/shard_map/ppermute | solution.py:362
  66.1 5.4 %collective-permute-start = (bf16[256,512]{1,0:T(8,128)(2,1)S(1)}, bf16[256,512]{1,0:T(8,128)(2,1)S(1)}, u32[]{:S(2)}, u32[]{:S(2)}) collective-permute-start(bf16[256,512]{1,0:T(8,128)(2,1)S(1)} %copy.18), channel_id=1, source_target_pairs={{0,32},{16,48},{32,0},{48,16},{1,33},{17,49},{33,1},{49,17},{2,34}... | collective-permute-start | bytes 786440 | tf_op jit(solution)/shard_map/ppermute | solution.py:362
  72.9 2.2 %collective-permute-done.1.refs_3_.refs_1_ = bf16[256,512]{1,0:T(8,128)(2,1)S(1)} collective-permute-done((bf16[256,512]{1,0:T(8,128)(2,1)S(1)}, bf16[256,512]{1,0:T(8,128)(2,1)S(1)}, u32[]{:S(2)}, u32[]{:S(2)}) %collective-permute-start.1) | collective-permute-done | bytes 262176 | tf_op jit(solution)/shard_map/ppermute | solution.py:362
  75.2 6.5 %collective-permute-done.refs_4_.q_ref = bf16[256,512]{1,0:T(8,128)(2,1)S(1)} collective-permute-done((bf16[256,512]{1,0:T(8,128)(2,1)S(1)}, bf16[256,512]{1,0:T(8,128)(2,1)S(1)}, u32[]{:S(2)}, u32[]{:S(2)}) %collective-permute-start) | collective-permute-done | bytes 262176 | tf_op jit(solution)/shard_map/ppermute | solution.py:362
  82.5 1.9 %collective-permute-start.3 = (bf16[1024,256]{1,0:T(8,128)(2,1)S(1)}, bf16[1024,256]{1,0:T(8,128)(2,1)S(1)}, u32[]{:S(2)}, u32[]{:S(2)}) collective-permute-start(bf16[1024,256]{1,0:T(8,128)(2,1)S(1)} %rebuild.1.mine_ref), channel_id=1, source_target_pairs={{0,1},{1,0},{2,3},{3,2},{4,5},{5,4},{6,7},{7,6},{8,9},{9,8},{10,11... | collective-permute-start | bytes 1572872 | tf_op jit(solution)/shard_map/ppermute | solution.py:362
  86.3 3.4 %attend.4 = (bf16[272,512]{1,0:T(8,128)(2,1)S(1)}, bf16[256,2048]{1,0:T(8,128)(2,1)S(1)}, bf16[2048,256]{1,0:T(8,128)(2,1)S(1)}) custom-call(s32[4]{0:T(128)S(1)} %pad_add_fusion.refs_0_.place_ref, bf16[256,512]{1,0:T(8,128)(2,1)S(1)} %collective-permute-done.refs_4_.q_ref, bf16[1024,256]{1,0:T(8,128)(2,1)S(1)} %rebuild.1.mine_ref, ...), custom_call_target="tpu_custom_call" | custom-call | flops 1073741824 | bytes 4194304 | tf_op jit(solution)/shard_map/attend/pallas_call | solution.py:499
  89.7 2.8 %collective-permute-start.4 = (bf16[272,512]{1,0:T(8,128)(2,1)S(1)}, bf16[272,512]{1,0:T(8,128)(2,1)S(1)}, u32[]{:S(2)}, u32[]{:S(2)}) collective-permute-start(bf16[272,512]{1,0:T(8,128)(2,1)S(1)} %get-tuple-element.21.refs_4_), channel_id=1, source_target_pairs={{0,32},{16,48},{32,0},{48,16},{1,33},{17,49},{33,1},{49,17},{2,34}... | collective-permute-start | bytes 835592 | tf_op jit(solution)/shard_map/ppermute | solution.py:362
  92.4 3.0 %attend.5.refs_4_ = bf16[272,512]{1,0:T(8,128)(2,1)S(1)} custom-call(s32[4]{0:T(128)S(1)} %pad_add_fusion.refs_0_.place_ref, bf16[256,512]{1,0:T(8,128)(2,1)S(1)} %collective-permute-done.1.refs_3_.refs_1_, bf16[256,2048]{1,0:T(8,128)(2,1)S(1)} %get-tuple-element.19.refs_2_, bf16[2048,256]{1,0:T(8,128)(2,1)S(1)} %get-tuple-element.20.refs_3_, ...), custom_call_target="tpu_custom_call" | custom-call | flops 1073741824 | bytes 4194304 | tf_op jit(solution)/shard_map/attend/pallas_call | solution.py:510
  95.5 3.0 %attend.6.refs_4_ = bf16[272,512]{1,0:T(8,128)(2,1)S(1)} custom-call(s32[4]{0:T(128)S(1)} %pad_add_fusion.refs_0_.place_ref, bf16[256,512]{1,0:T(8,128)(2,1)S(1)} %collective-permute-done.2.refs_5_.refs_1_, bf16[256,2048]{1,0:T(8,128)(2,1)S(1)} %get-tuple-element.19.refs_2_, bf16[2048,256]{1,0:T(8,128)(2,1)S(1)} %get-tuple-element.20.refs_3_, ...), custom_call_target="tpu_custom_call" | custom-call | flops 1073741824 | bytes 4194304 | tf_op jit(solution)/shard_map/attend/pallas_call | solution.py:510
  98.5 4.3 %collective-permute-start.6 = (bf16[272,512]{1,0:T(8,128)(2,1)S(1)}, bf16[272,512]{1,0:T(8,128)(2,1)S(1)}, u32[]{:S(2)}, u32[]{:S(2)}) collective-permute-start(bf16[272,512]{1,0:T(8,128)(2,1)S(1)} %attend.6.refs_4_), channel_id=1, source_target_pairs={{0,48},{16,32},{32,16},{48,0},{1,49},{17,33},{33,17},{49,1},{2,50}... | collective-permute-start | bytes 835592 | tf_op jit(solution)/shard_map/ppermute | solution.py:362
  102.9 2.3 %collective-permute-start.5 = (bf16[272,512]{1,0:T(8,128)(2,1)S(1)}, bf16[272,512]{1,0:T(8,128)(2,1)S(1)}, u32[]{:S(2)}, u32[]{:S(2)}) collective-permute-start(bf16[272,512]{1,0:T(8,128)(2,1)S(1)} %attend.5.refs_4_), channel_id=1, source_target_pairs={{0,16},{16,0},{32,48},{48,32},{1,17},{17,1},{33,49},{49,33},{2,18}... | collective-permute-start | bytes 835592 | tf_op jit(solution)/shard_map/ppermute | solution.py:362
  105.2 3.1 %attend.7.own_ref = bf16[272,512]{1,0:T(8,128)(2,1)S(1)} custom-call(s32[4]{0:T(128)S(1)} %pad_add_fusion.refs_0_.place_ref, bf16[256,512]{1,0:T(8,128)(2,1)S(1)} %copy-done, bf16[256,2048]{1,0:T(8,128)(2,1)S(1)} %get-tuple-element.19.refs_2_, bf16[2048,256]{1,0:T(8,128)(2,1)S(1)} %get-tuple-element.20.refs_3_, bf16[272,512]{1,0:T(8,128)(2,1)S(1)} %attend.6.refs_4_, ...), custom_call_target="tpu_custom_call" | custom-call | flops 1073741824 | bytes 4194304 | tf_op jit(solution)/shard_map/attend/pallas_call | solution.py:510
  110.0 2.9 %collective-permute-done.5.back1_ref = bf16[272,512]{1,0:T(8,128)(2,1)S(1)} collective-permute-done((bf16[272,512]{1,0:T(8,128)(2,1)S(1)}, bf16[272,512]{1,0:T(8,128)(2,1)S(1)}, u32[]{:S(2)}, u32[]{:S(2)}) %collective-permute-start.5) | collective-permute-done | bytes 278560 | tf_op jit(solution)/shard_map/ppermute | solution.py:362
  (42 shorter events, 10.7 us)
Async XLA Ops:
  0.6 7.0 %copy-start.11 = (bf16[256,512]{1,0:T(8,128)(2,1)S(1)}, bf16[256,512]{1,0:T(8,128)(2,1)}, u32[]{:S(2)}) copy-start(bf16[256,512]{1,0:T(8,128)(2,1)} %refs_0_.4) | copy-start | bytes 786436
  0.6 7.0 %copy-start.12 = (bf16[512,256]{1,0:T(8,128)(2,1)S(1)}, bf16[512,256]{1,0:T(8,128)(2,1)}, u32[]{:S(2)}) copy-start(bf16[512,256]{1,0:T(8,128)(2,1)} %refs_1_.3) | copy-start | bytes 786436
  3.2 4.4 %copy-start.1 = (bf16[4,16,1152]{2,1,0:T(8,128)(2,1)S(1)}, bf16[4,16,1152]{2,1,0:T(8,128)(2,1)}, u32[]{:S(2)}) copy-start(bf16[4,16,1152]{2,1,0:T(8,128)(2,1)} %state.1.refs_2_) | copy-start | bytes 442372
  3.2 10.5 %all-to-all-start = ((bf16[4,16,1152]{2,1,0:T(8,128)(2,1)}), bf16[4,16,1152]{2,1,0:T(8,128)(2,1)S(1)}, u32[]{:S(2)}, u32[]{:S(2)}) async-start(bf16[4,16,1152]{2,1,0:T(8,128)(2,1)} %state.1.refs_2_), calls=%async_computation | async-start | bytes 294912 | tf_op jit(solution)/shard_map/all_to_all | solution.py:366
  7.9 15.5 %copy-start.3 = (bf16[256,1024]{1,0:T(8,128)(2,1)S(1)}, bf16[256,1024]{1,0:T(8,128)(2,1)}, u32[]{:S(2)}) copy-start(bf16[256,1024]{1,0:T(8,128)(2,1)} %refs_2_.1) | copy-start | bytes 1572868
  15.2 8.2 %copy-start.4 = (f32[16,256]{1,0:T(8,128)S(1)}, f32[16,256]{1,0:T(8,128)}, u32[]{:S(2)}) copy-start(f32[16,256]{1,0:T(8,128)} %refs_3_.1) | copy-start | bytes 49156
  15.2 8.2 %copy-start.5 = (bf16[16,256]{1,0:T(8,128)(2,1)S(1)}, bf16[16,256]{1,0:T(8,128)(2,1)}, u32[]{:S(2)}) copy-start(bf16[16,256]{1,0:T(8,128)(2,1)} %refs_4_.1) | copy-start | bytes 24580
  15.2 8.2 %copy-start.6 = (bf16[16,256]{1,0:T(8,128)(2,1)S(1)}, bf16[16,256]{1,0:T(8,128)(2,1)}, u32[]{:S(2)}) copy-start(bf16[16,256]{1,0:T(8,128)(2,1)} %c_ref.1) | copy-start | bytes 24580
  15.2 16.6 %all-to-all-start.1 = ((bf16[8,16,1152]{2,1,0:T(8,128)(2,1)}), bf16[8,16,1152]{2,1,0:T(8,128)(2,1)S(1)}, u32[]{:S(2)}, u32[]{:S(2)}) async-start(bf16[8,16,1152]{2,1,0:T(8,128)(2,1)} %get-tuple-element.12), calls=%async_computation.1 | async-start | bytes 589824 | tf_op jit(solution)/shard_map/all_to_all | solution.py:366
  23.4 0.7 copy-start.13
  24.0 7.8 %copy-start.2 = (bf16[1024,256]{1,0:T(8,128)(2,1)S(1)}, bf16[1024,256]{1,0:T(8,128)(2,1)}, u32[]{:S(2)}) copy-start(bf16[1024,256]{1,0:T(8,128)(2,1)} %w_ref.1) | copy-start | bytes 1572868
  26.3 5.5 %copy-start.7 = (f32[1024]{0:T(1024)S(1)}, f32[1024]{0:T(1024)}, u32[]{:S(2)}) copy-start(f32[1024]{0:T(1024)} %param.20) | copy-start | bytes 12292
  34.4 9.9 %copy-start = (bf16[256,512]{1,0:T(8,128)(2,1)S(1)}, bf16[256,512]{1,0:T(8,128)(2,1)}, u32[]{:S(2)}) copy-start(bf16[256,512]{1,0:T(8,128)(2,1)} %refs_1_.5) | copy-start | bytes 786436
  34.4 18.7 %all-to-all-start.2 = ((bf16[16,16,256]{2,1,0:T(8,128)(2,1)}), bf16[16,16,256]{2,1,0:T(8,128)(2,1)S(1)}, u32[]{:S(2)}, u32[]{:S(2)}) async-start(bf16[16,16,256]{2,1,0:T(8,128)(2,1)} %bitcast.5), calls=%async_computation.2 | async-start | bytes 262144 | tf_op jit(solution)/shard_map/all_to_all | solution.py:366
  54.0 27.7 %all-to-all-start.3 = ((bf16[64,16,256]{2,1,0:T(8,128)(2,1)}), bf16[64,16,256]{2,1,0:T(8,128)(2,1)S(1)}, u32[]{:S(2)}, u32[]{:S(2)}) async-start(bf16[64,16,256]{2,1,0:T(8,128)(2,1)} %sum.1.refs_1_.order_ref), calls=%async_computation.3 | async-start | bytes 1048576 | tf_op jit(solution)/shard_map/all_to_all | solution.py:366
  60.9 10.6 %copy-start.9 = (bf16[256,1024]{1,0:T(8,128)(2,1)S(1)}, bf16[256,1024]{1,0:T(8,128)(2,1)}, u32[]{:S(2)}) copy-start(bf16[256,1024]{1,0:T(8,128)(2,1)} %wk_ref.1) | copy-start | bytes 1572868
  60.9 10.6 %copy-start.10 = (bf16[256,1024]{1,0:T(8,128)(2,1)S(1)}, bf16[256,1024]{1,0:T(8,128)(2,1)}, u32[]{:S(2)}) copy-start(bf16[256,1024]{1,0:T(8,128)(2,1)} %wv_ref.1) | copy-start | bytes 1572868
  60.9 12.0 %collective-permute-start.2 = (bf16[256,512]{1,0:T(8,128)(2,1)S(1)}, bf16[256,512]{1,0:T(8,128)(2,1)S(1)}, u32[]{:S(2)}, u32[]{:S(2)}) collective-permute-start(bf16[256,512]{1,0:T(8,128)(2,1)S(1)} %copy.18), channel_id=1, source_target_pairs={{0,48},{16,32},{32,16},{48,0},{1,49},{17,33},{33,17},{49,1},{2,50}... | collective-permute-start | bytes 786440 | tf_op jit(solution)/shard_map/ppermute | solution.py:362
  64.1 11.0 %collective-permute-start.1 = (bf16[256,512]{1,0:T(8,128)(2,1)S(1)}, bf16[256,512]{1,0:T(8,128)(2,1)S(1)}, u32[]{:S(2)}, u32[]{:S(2)}) collective-permute-start(bf16[256,512]{1,0:T(8,128)(2,1)S(1)} %copy.18), channel_id=1, source_target_pairs={{0,16},{16,0},{32,48},{48,32},{1,17},{17,1},{33,49},{49,33},{2,18}... | collective-permute-start | bytes 786440 | tf_op jit(solution)/shard_map/ppermute | solution.py:362
  66.1 15.6 %collective-permute-start = (bf16[256,512]{1,0:T(8,128)(2,1)S(1)}, bf16[256,512]{1,0:T(8,128)(2,1)S(1)}, u32[]{:S(2)}, u32[]{:S(2)}) collective-permute-start(bf16[256,512]{1,0:T(8,128)(2,1)S(1)} %copy.18), channel_id=1, source_target_pairs={{0,32},{16,48},{32,0},{48,16},{1,33},{17,49},{33,1},{49,17},{2,34}... | collective-permute-start | bytes 786440 | tf_op jit(solution)/shard_map/ppermute | solution.py:362
  82.5 3.8 %collective-permute-start.3 = (bf16[1024,256]{1,0:T(8,128)(2,1)S(1)}, bf16[1024,256]{1,0:T(8,128)(2,1)S(1)}, u32[]{:S(2)}, u32[]{:S(2)}) collective-permute-start(bf16[1024,256]{1,0:T(8,128)(2,1)S(1)} %rebuild.1.mine_ref), channel_id=1, source_target_pairs={{0,1},{1,0},{2,3},{3,2},{4,5},{5,4},{6,7},{7,6},{8,9},{9,8},{10,11... | collective-permute-start | bytes 1572872 | tf_op jit(solution)/shard_map/ppermute | solution.py:362
  89.7 15.5 %collective-permute-start.4 = (bf16[272,512]{1,0:T(8,128)(2,1)S(1)}, bf16[272,512]{1,0:T(8,128)(2,1)S(1)}, u32[]{:S(2)}, u32[]{:S(2)}) collective-permute-start(bf16[272,512]{1,0:T(8,128)(2,1)S(1)} %get-tuple-element.21.refs_4_), channel_id=1, source_target_pairs={{0,32},{16,48},{32,0},{48,16},{1,33},{17,49},{33,1},{49,17},{2,34}... | collective-permute-start | bytes 835592 | tf_op jit(solution)/shard_map/ppermute | solution.py:362
  98.5 11.5 %collective-permute-start.6 = (bf16[272,512]{1,0:T(8,128)(2,1)S(1)}, bf16[272,512]{1,0:T(8,128)(2,1)S(1)}, u32[]{:S(2)}, u32[]{:S(2)}) collective-permute-start(bf16[272,512]{1,0:T(8,128)(2,1)S(1)} %attend.6.refs_4_), channel_id=1, source_target_pairs={{0,48},{16,32},{32,16},{48,0},{1,49},{17,33},{33,17},{49,1},{2,50}... | collective-permute-start | bytes 835592 | tf_op jit(solution)/shard_map/ppermute | solution.py:362
  102.9 10.0 %collective-permute-start.5 = (bf16[272,512]{1,0:T(8,128)(2,1)S(1)}, bf16[272,512]{1,0:T(8,128)(2,1)S(1)}, u32[]{:S(2)}, u32[]{:S(2)}) collective-permute-start(bf16[272,512]{1,0:T(8,128)(2,1)S(1)} %attend.5.refs_4_), channel_id=1, source_target_pairs={{0,16},{16,0},{32,48},{48,32},{1,17},{17,1},{33,49},{49,33},{2,18}... | collective-permute-start | bytes 835592 | tf_op jit(solution)/shard_map/ppermute | solution.py:362
  (1 other events, 0.7 us)
